TPU v7x, 32 devices: a whole 2x2x4 slice. The times are simulated.
32 devices in a mesh: slides: 1, row: 16 (over z, y, x), col: 2 (over core).
Axes of the slice: x: 2, y: 2, z: 4, core: 2. Of those that a mesh axis runs over, the one named last changes fastest.
Arguments:
- image: bfloat16 [64, 128, 768], P(('slides', 'row'), 'col'), may hold values from -6 to 6
- dw_kernel: float32 [49, 768], replicated, may hold values from -0.875 to 0.875
- w_in: bfloat16 [768, 3072], replicated, may hold values from -0.21875 to 0.21875
- w_out: bfloat16 [3072, 768], replicated, may hold values from -0.109375 to 0.109375
- layer_scale: float32 [768], replicated, may hold values from 0.5 to 1.5
- region_ids: int32 [32, 64], P(('slides', 'row'), 'col'), may hold values from 0 to 127, as said below
- region_slot: int32 [128], P('slides'), may hold values from 0 to 127, each once
- pool_grad: bfloat16 [128, 768], P(('slides', 'row', 'col')), may hold values from -6 to 6
Outputs:
- region_pool: float32 [128, 768], P(('slides', 'row', 'col'))
- grad_image: bfloat16 [64, 128, 768], P(('slides', 'row'), 'col')
- grad_w_in: float32 [768, 3072], P('slides', ('row', 'col'))
- grad_w_out: float32 [3072, 768], P(('slides', 'row', 'col'))
- grad_kernel: float32 [49, 768], P('slides')
Inputs may be any that keep to these rules, and one draw needn't show every extreme that they name: `region_ids`: every region is named by some tile. `region_slot`: each slot once; slot s lies on index s // 4 of row+col.
All inputs are finite; a program needn't handle non-finite values.
Results may differ from a plain program's by a relative error of at most 0.007.
Values may be sent and summed in bfloat16 or wider, within the bound.
A program may use at most 192 MiB of HBM per device.

v0:
```python
import math

import jax
import jax.numpy as jnp
from jax import lax
from jax.sharding import PartitionSpec as P


def extended(cells, sides, width):
    for axis, dim in sides:
        count = lax.axis_size(axis)
        ends = count - 1
        head = lax.slice_in_dim(cells, 0, width, axis=dim)
        tail = lax.slice_in_dim(cells, cells.shape[dim] - width, cells.shape[dim], axis=dim)
        cells = jnp.concatenate(
            [
                lax.ppermute(tail, axis, [(i, (i + 1) % count) for i in range(ends)]),
                cells,
                lax.ppermute(head, axis, [((i + 1) % count, i) for i in range(ends)]),
            ],
            axis=dim,
        )
    return cells


def widen(field, forward):
    if forward:
        return extended(field, (("row", 0), ("col", 1)), 3)
    return extended(field.astype(jnp.bfloat16), (("row", 0), ("col", 1)), 3).astype(field.dtype)


def depthwise(padded, taps, height, breadth, flipped):
    total = jnp.zeros((height, breadth, padded.shape[2]), jnp.float32)
    for a in range(7):
        if flipped:
            terms = [
                padded[6 - a : 6 - a + height, 6 - b : 6 - b + breadth] * taps[a, b]
                for b in range(7)
            ]
        else:
            terms = [padded[a : a + height, b : b + breadth] * taps[a, b] for b in range(7)]
        row_total = terms[0]
        for term in terms[1:]:
            row_total = row_total + term
        total = total + row_total
    return total


def shards(image, dw_kernel, w_in, w_out, layer_scale, region_ids, region_slot, pool_grad):
    height, breadth, width = image.shape
    taps = dw_kernel.reshape(7, 7, width)
    xfull = image.astype(jnp.float32)
    xpad = widen(image, True).astype(jnp.float32)
    conv = depthwise(xpad, taps, height, breadth, False)
    centre = conv - jnp.mean(conv, axis=-1, keepdims=True)
    inv_std = lax.rsqrt(jnp.mean(centre * centre, axis=-1, keepdims=True) + 1e-06)
    normed_f = centre * inv_std
    normed = normed_f.astype(jnp.bfloat16).reshape(-1, width)
    pre = jnp.dot(normed, w_in, preferred_element_type=jnp.float32)
    hidden = jax.nn.gelu(pre, approximate=False).astype(jnp.bfloat16)
    branch = jnp.dot(hidden, w_out, preferred_element_type=jnp.float32).reshape(
        height, breadth, width
    )
    block = (xfull + layer_scale * branch).astype(jnp.bfloat16)
    tile_sum = (
        block.astype(jnp.float32)
        .reshape(height // 2, 2, breadth // 2, 2, width)
        .sum(axis=(1, 3))
        .reshape(-1, width)
    )
    regions = region_slot.shape[0]
    labels = region_ids.reshape(-1)
    region_iota = jnp.arange(regions, dtype=jnp.int32)
    id_onehot = (labels[:, None] == region_iota[None, :]).astype(jnp.bfloat16)
    slot_onehot = (region_slot[:, None] == region_iota[None, :]).astype(jnp.bfloat16)
    tile_onehot = jnp.dot(id_onehot, slot_onehot, preferred_element_type=jnp.float32)
    partial_sum = jnp.dot(
        tile_onehot.T, tile_sum, precision=lax.Precision.HIGHEST, preferred_element_type=jnp.float32
    )
    partial_count = jnp.sum(tile_onehot, axis=0)
    owned_sum, owned_count = (
        lax.psum_scatter(partial_sum, ("row", "col"), scatter_dimension=0, tiled=True),
        lax.psum_scatter(partial_count, ("row", "col"), scatter_dimension=0, tiled=True),
    )
    region_pool = owned_sum / (4.0 * owned_count)[:, None]
    region_grad = (pool_grad.astype(jnp.float32) / (4.0 * owned_count)[:, None]).astype(
        jnp.bfloat16
    )
    every_grad = lax.all_gather(region_grad, ("row", "col"), axis=0, tiled=True)
    tile_grad = jnp.dot(
        tile_onehot.astype(jnp.bfloat16), every_grad, preferred_element_type=jnp.float32
    )
    tile_grad = tile_grad.reshape(height // 2, 1, breadth // 2, 1, width)
    dblock = jnp.broadcast_to(tile_grad, (height // 2, 2, breadth // 2, 2, width)).reshape(
        height, breadth, width
    )
    g_out = (dblock * layer_scale).astype(jnp.bfloat16).reshape(-1, width)
    dhidden = jnp.dot(g_out, w_out.T, preferred_element_type=jnp.float32)
    cdf = 0.5 * (1.0 + lax.erf(pre / math.sqrt(2.0)))
    density = jnp.exp(-0.5 * pre * pre) / math.sqrt(2.0 * math.pi)
    g_in = (dhidden * (cdf + pre * density)).astype(jnp.bfloat16)
    full_out = jnp.dot(hidden.T, g_out, preferred_element_type=jnp.float32)
    full_in = jnp.dot(normed.T, g_in, preferred_element_type=jnp.float32)
    grad_w_in, grad_w_out = (
        lax.psum_scatter(full_in, ("row", "col"), scatter_dimension=1, tiled=True),
        lax.psum_scatter(full_out, ("row", "col"), scatter_dimension=0, tiled=True),
    )
    dnorm = jnp.dot(g_in, w_in.T, preferred_element_type=jnp.float32).reshape(
        height, breadth, width
    )
    dconv = inv_std * (
        dnorm
        - jnp.mean(dnorm, axis=-1, keepdims=True)
        - normed_f * jnp.mean(dnorm * normed_f, axis=-1, keepdims=True)
    )
    dpad = widen(dconv, False)
    back = depthwise(dpad, taps, height, breadth, True)
    kernel_rows = []
    for a in range(7):
        for b in range(7):
            kernel_rows.append(jnp.sum(xpad[a : a + height, b : b + breadth] * dconv, axis=(0, 1)))
    grad_kernel = lax.psum(jnp.stack(kernel_rows, axis=0), ("row", "col"))
    grad_image = (dblock + back).astype(jnp.bfloat16)
    return (region_pool, grad_image, grad_w_in, grad_w_out, grad_kernel)


def solution(mesh):
    placed = (
        P(("slides", "row"), "col", None),
        P(),
        P(),
        P(),
        P(),
        P(("slides", "row"), "col"),
        P("slides"),
        P(("slides", "row", "col"), None),
    )
    return jax.shard_map(
        shards,
        mesh=mesh,
        in_specs=placed,
        out_specs=(
            P(("slides", "row", "col"), None),
            P(("slides", "row"), "col", None),
            P("slides", ("row", "col")),
            P(("slides", "row", "col"), None),
            P("slides", None),
        ),
        check_vma=False,
    )
```

profile of v0, /device:TPU:0, one launch (start us, length us, event | category | flops | bytes accessed | tf_op | source)
XLA Modules:
  0.0 566.9 jit_solution(408561282894542323)
XLA Ops:
  7.2 1.1 fusion.79
  8.4 1.3 collective-permute-start.1
  9.7 5.5 collective-permute-start
  15.2 0.8 eq.28
  15.9 0.9 fusion.80
  16.8 44.4 %all-reduce.1 = f32[128]{0:T(128)S(1)} all-reduce(f32[128]{0:T(128)S(1)} %get-tuple-element.119), channel_id=3, replica_groups=mesh['slides'=1,'row'=16,'col'=2] {'row','col'}, use_global_device_ids=true, to_apply=%region_5.0.clone | all-reduce | flops 128 | bytes 1024
  61.3 0.8 fusion.74
  62.1 40.2 %all-gather = bf16[32,4,768]{2,1,0:T(4,128)(2,1)S(1)} all-gather(bf16[1,4,768]{2,1,0:T(4,128)(2,1)S(1)} %fusion.74), channel_id=1, replica_groups=mesh['slides'=1,'row'=16,'col'=2] {'row','col'}, dimensions={0}, use_global_device_ids=true | all-gather | bytes 202752 | tf_op jit(solution)/shard_map/all_gather | solution.py:89
  102.5 0.9 reshape.70
  103.6 0.7 slice_reduce_fusion.47
  104.6 2.3 collective-permute-start.2
  106.8 1.5 collective-permute-start.3
  108.8 1.4 reshape.77
  110.2 1.6 maximum_convert_fusion
  111.9 6.0 %fusion.76 = (f32[4,64]{1,0:T(4,128)S(1)}, f32[4,64,768]{2,1,0:T(8,128)S(1)}) fusion(f32[768]{0:T(1024)S(1)} %get-tuple-element.55, f32[10,70,768]{2,1,0:T(8,128)S(1)} %maximum_convert_fusion, f32[768]{0:T(1024)S(1)} %get-tuple-element.56, f32[768]{0:T(1024)S(1)} %get-tuple-element.57, f32[768]{0:T(1024)S(1)} %get-tuple-element.58, ...), kind=kLoop, calls=%fused_computation.258 | loop fusion | flops 19267328 | bytes 39473152 | tf_op jit(solution)/shard_map/reduce_sum | solution.py:55
  118.5 0.4 copy-done.50
  119.0 9.0 %fusion.3 = (bf16[256,3072]{1,0:T(8,128)(2,1)}, f32[256,3072]{1,0:T(8,128)S(1)}) fusion(bf16[256,768]{1,0:T(8,128)(2,1)S(1)} %bitcast.23, bf16[768,3072]{1,0:T(8,128)(2,1)S(1)} %bitcast.29), kind=kOutput, calls=%fused_computation.6 | convolution fusion | flops 1259077632 | bytes 9830400 | tf_op jit(solution)/shard_map/dot_general | solution.py:59
  128.0 2.0 fusion
  130.0 2.4 fusion.81
  132.5 0.7 div.47
  133.2 1.4 multiply_reduce_fusion.49
  134.6 1.4 fusion.75
  135.9 1.1 multiply_reduce_fusion.36
  137.1 1.9 multiply_reduce_fusion
  139.0 2.1 multiply_reduce_fusion.18
  141.1 1.4 fusion.82
  142.7 0.5 reshape.80
  143.1 0.5 reduce_sum.497
  143.7 1.3 fusion.83
  145.5 4.5 stack.199
  150.1 5.1 fusion.67
  155.3 0.9 copy-done.10
  156.2 0.5 copy-done.12
  156.7 5.1 fusion.84
  162.1 1.4 collective-permute-start.4
  163.5 1.3 collective-permute-start.5
  164.9 0.5 reshape.76
  165.4 11.6 %collective-permute-done.4 = bf16[3,64,768]{2,1,0:T(8,128)(2,1)S(1)} collective-permute-done((bf16[3,64,768]{2,1,0:T(8,128)(2,1)S(1)}, bf16[3,64,768]{2,1,0:T(8,128)(2,1)S(1)}, u32[]{:S(2)}, u32[]{:S(2)}) %collective-permute-start.4) | collective-permute-done | bytes 294944 | tf_op jit(solution)/shard_map/ppermute | solution.py:17
  177.0 0.8 collective-permute-done.5
  177.8 2.0 collective-permute-start.6
  179.8 1.3 collective-permute-start.7
  181.1 93.4 %all-reduce.5.cloned.1.call-done = (f32[128,768]{1,0:T(8,128)}, f32[49,768]{1,0:T(8,128)}) async-done(((f32[128,768]{1,0:T(8,128)}, f32[49,768]{1,0:T(8,128)}), (f32[128,768]{1,0:T(8,128)}, f32[49,768]{1,0:T(8,128)})) %all-reduce.5.cloned.1.call-update) | async-done | bytes 543760
  274.5 1.4 dynamic-slice_divide_fusion
  275.9 0.3 maximum_convert_fusion.1
  276.4 6.5 %fusion.18 = bf16[4,64,768]{2,1,0:T(8,128)(2,1)} fusion(f32[4,64,768]{2,1,0:T(8,128)S(1)} %reshape.76, f32[10,70,768]{2,1,0:T(8,128)S(1)} %maximum_convert_fusion.1, f32[768]{0:T(1024)S(1)} %get-tuple-element.55, f32[768]{0:T(1024)S(1)} %get-tuple-element.56, f32[768]{0:T(1024)S(1)} %get-tuple-element.57, f32[768]{0:T(1024)S(1)} %get-tuple-element.58, ...), kind=kLoop, calls=%fused_computation.32 | loop fusion | flops 19464192 | bytes 39865344 | tf_op jit(solution)/shard_map/convert_element_type | solution.py:123
  282.9 135.4 %reduce-scatter.5.cloned.1.call-done = f32[96,768]{1,0:T(8,128)} async-done(((f32[3072,768]{1,0:T(8,128)}), f32[96,768]{1,0:T(8,128)}) %reduce-scatter.5.cloned.1.call-update) | async-done | bytes 294928 | tf_op jit(solution)/shard_map/reduce_scatter | solution.py:106
  418.3 141.4 %reduce-scatter.3.cloned.1.call-done = f32[768,96]{0,1:T(8,128)} async-done(((f32[768,3072]{0,1:T(8,128)}), f32[768,96]{0,1:T(8,128)}) %reduce-scatter.3.cloned.1.call-update) | async-done | bytes 294928 | tf_op jit(solution)/shard_map/reduce_scatter | solution.py:105
  559.7 0.7 copy.17
  (204 shorter events, 2.1 us)
Async XLA Ops:
  7.2 97.2 %copy-start.2 = (bf16[4,64,768]{2,1,0:T(8,128)(2,1)S(1)}, bf16[4,64,768]{2,1,0:T(8,128)(2,1)}, u32[]{:S(2)}) copy-start(bf16[4,64,768]{2,1,0:T(8,128)(2,1)} %param.8) | copy-start | bytes 1179652
  7.2 267.3 %all-reduce.5.cloned.1.call-start = ((), (), s32[]{:S(2)}) async-start(), calls=%async_computation.4 | async-start | bytes 1130496
  8.4 96.1 %collective-permute-start.1 = (bf16[3,64,768]{2,1,0:T(8,128)(2,1)S(1)}, bf16[3,64,768]{2,1,0:T(8,128)(2,1)S(1)}, u32[]{:S(2)}, u32[]{:S(2)}) collective-permute-start(bf16[3,64,768]{2,1,0:T(8,128)(2,1)S(1)} %get-tuple-element.115), channel_id=1, source_target_pairs={{2,0},{4,2},{6,4},{8,6},{10,8},{12,10},{14,12},{16,14},{18,16},{20... | collective-permute-start | bytes 884744 | tf_op jit(solution)/shard_map/ppermute | solution.py:19
  9.7 94.7 %collective-permute-start = (bf16[3,64,768]{2,1,0:T(8,128)(2,1)S(1)}, bf16[3,64,768]{2,1,0:T(8,128)(2,1)S(1)}, u32[]{:S(2)}, u32[]{:S(2)}) collective-permute-start(bf16[3,64,768]{2,1,0:T(8,128)(2,1)S(1)} %get-tuple-element.116), channel_id=1, source_target_pairs={{0,2},{2,4},{4,6},{6,8},{8,10},{10,12},{12,14},{14,16},{16,18},{18... | collective-permute-start | bytes 884744 | tf_op jit(solution)/shard_map/ppermute | solution.py:17
  104.6 5.6 collective-permute-start.2
  106.8 3.4 collective-permute-start.3
  108.4 9.6 %copy-start.28 = (f32[768]{0:T(1024)}, f32[768]{0:T(1024)S(1)}, u32[]{:S(2)}) copy-start(f32[768]{0:T(1024)S(1)} %get-tuple-element.92) | copy-start | bytes 9220
  108.4 9.5 %copy-start.30 = (f32[768]{0:T(1024)}, f32[768]{0:T(1024)S(1)}, u32[]{:S(2)}) copy-start(f32[768]{0:T(1024)S(1)} %get-tuple-element.93) | copy-start | bytes 9220
  108.5 9.5 %copy-start.32 = (f32[768]{0:T(1024)}, f32[768]{0:T(1024)S(1)}, u32[]{:S(2)}) copy-start(f32[768]{0:T(1024)S(1)} %get-tuple-element.94) | copy-start | bytes 9220
  108.5 9.5 %copy-start.34 = (f32[768]{0:T(1024)}, f32[768]{0:T(1024)S(1)}, u32[]{:S(2)}) copy-start(f32[768]{0:T(1024)S(1)} %get-tuple-element.95) | copy-start | bytes 9220
  108.5 9.5 %copy-start.36 = (f32[768]{0:T(1024)}, f32[768]{0:T(1024)S(1)}, u32[]{:S(2)}) copy-start(f32[768]{0:T(1024)S(1)} %get-tuple-element.96) | copy-start | bytes 9220
  108.5 9.5 %copy-start.38 = (f32[768]{0:T(1024)}, f32[768]{0:T(1024)S(1)}, u32[]{:S(2)}) copy-start(f32[768]{0:T(1024)S(1)} %get-tuple-element.97) | copy-start | bytes 9220
  108.5 9.5 %copy-start.40 = (f32[768]{0:T(1024)}, f32[768]{0:T(1024)S(1)}, u32[]{:S(2)}) copy-start(f32[768]{0:T(1024)S(1)} %get-tuple-element.98) | copy-start | bytes 9220
  108.5 9.5 %copy-start.42 = (f32[768]{0:T(1024)}, f32[768]{0:T(1024)S(1)}, u32[]{:S(2)}) copy-start(f32[768]{0:T(1024)S(1)} %get-tuple-element.99) | copy-start | bytes 9220
  108.5 9.5 %copy-start.44 = (f32[768]{0:T(1024)}, f32[768]{0:T(1024)S(1)}, u32[]{:S(2)}) copy-start(f32[768]{0:T(1024)S(1)} %get-tuple-element.100) | copy-start | bytes 9220
  108.5 9.5 %copy-start.46 = (f32[768]{0:T(1024)}, f32[768]{0:T(1024)S(1)}, u32[]{:S(2)}) copy-start(f32[768]{0:T(1024)S(1)} %get-tuple-element.101) | copy-start | bytes 9220
  108.5 9.5 %copy-start.48 = (f32[768]{0:T(1024)}, f32[768]{0:T(1024)S(1)}, u32[]{:S(2)}) copy-start(f32[768]{0:T(1024)S(1)} %get-tuple-element.102) | copy-start | bytes 9220
  118.1 9.9 %slice-start.2 = ((s8[4718592]{0:T(1024)(128)(4,1)}), s8[4194304]{0:T(1024)(128)(4,1)S(1)}, s32[]{:S(2)}) async-start(s8[4718592]{0:T(1024)(128)(4,1)} %bitcast.30), calls=%async_computation.7 | async-start | bytes 8388608
  118.9 9.0 %copy-start.9 = (bf16[4,64,768]{2,1,0:T(8,128)(2,1)}, bf16[4,64,768]{2,1,0:T(8,128)(2,1)S(1)}, u32[]{:S(2)}) copy-start(bf16[4,64,768]{2,1,0:T(8,128)(2,1)S(1)} %fusion.65) | copy-start | bytes 1179652
  118.9 9.0 %copy-start.4 = (f32[256,768]{1,0:T(8,128)S(1)}, f32[256,768]{1,0:T(8,128)}, u32[]{:S(2)}) copy-start(f32[256,768]{1,0:T(8,128)} %reshape.77) | copy-start | bytes 2359300
  118.9 9.0 %copy-start.52 = (f32[768]{0:T(1024)S(1)}, f32[768]{0:T(1024)}, u32[]{:S(2)}) copy-start(f32[768]{0:T(1024)} %param.12) | copy-start | bytes 9220
  119.0 9.0 %slice-start.3 = ((s8[4718592]{0:T(1024)(128)(4,1)}), s8[524288]{0:T(1024)(128)(4,1)S(1)}, s32[]{:S(2)}) async-start(s8[4718592]{0:T(1024)(128)(4,1)} %bitcast.30), calls=%async_computation.8 | async-start | bytes 1048576
  150.1 268.3 %reduce-scatter.5.cloned.1.call-start = ((), (), s32[]{:S(2)}) async-start(), calls=%async_computation.3 | async-start | bytes 9732096 | tf_op jit(solution)/shard_map/reduce_scatter | solution.py:106
  155.2 404.5 %reduce-scatter.3.cloned.1.call-start = ((), (), s32[]{:S(2)}) async-start(), calls=%async_computation.2 | async-start | bytes 9732096 | tf_op jit(solution)/shard_map/reduce_scatter | solution.py:105
  161.9 112.6 %copy-start.55 = (f32[4]{0:T(128)S(1)}, f32[4]{0:T(128)}, u32[]{:S(2)}) copy-start(f32[4]{0:T(128)} %copy-done.54) | copy-start | bytes 52
  161.9 114.3 %copy-start.15 = (f32[768]{0:T(1024)S(1)}, f32[768]{0:T(1024)}, u32[]{:S(2)}) copy-start(f32[768]{0:T(1024)} %copy-done.14) | copy-start | bytes 9220
  161.9 114.3 %copy-start.17 = (f32[768]{0:T(1024)S(1)}, f32[768]{0:T(1024)}, u32[]{:S(2)}) copy-start(f32[768]{0:T(1024)} %get-tuple-element.86) | copy-start | bytes 9220
  161.9 114.3 %copy-start.19 = (f32[768]{0:T(1024)S(1)}, f32[768]{0:T(1024)}, u32[]{:S(2)}) copy-start(f32[768]{0:T(1024)} %get-tuple-element.87) | copy-start | bytes 9220
  161.9 114.3 %copy-start.21 = (f32[768]{0:T(1024)S(1)}, f32[768]{0:T(1024)}, u32[]{:S(2)}) copy-start(f32[768]{0:T(1024)} %get-tuple-element.88) | copy-start | bytes 9220
  162.0 114.3 %copy-start.23 = (f32[768]{0:T(1024)S(1)}, f32[768]{0:T(1024)}, u32[]{:S(2)}) copy-start(f32[768]{0:T(1024)} %get-tuple-element.89) | copy-start | bytes 9220
  162.0 114.3 %copy-start.25 = (f32[768]{0:T(1024)S(1)}, f32[768]{0:T(1024)}, u32[]{:S(2)}) copy-start(f32[768]{0:T(1024)} %get-tuple-element.90) | copy-start | bytes 9220
  162.0 114.3 %copy-start.27 = (f32[768]{0:T(1024)S(1)}, f32[768]{0:T(1024)}, u32[]{:S(2)}) copy-start(f32[768]{0:T(1024)} %get-tuple-element.91) | copy-start | bytes 9220
  162.0 114.3 %copy-start.29 = (f32[768]{0:T(1024)S(1)}, f32[768]{0:T(1024)}, u32[]{:S(2)}) copy-start(f32[768]{0:T(1024)} %copy-done.28) | copy-start | bytes 9220
  162.0 114.3 %copy-start.31 = (f32[768]{0:T(1024)S(1)}, f32[768]{0:T(1024)}, u32[]{:S(2)}) copy-start(f32[768]{0:T(1024)} %copy-done.30) | copy-start | bytes 9220
  162.0 114.3 %copy-start.33 = (f32[768]{0:T(1024)S(1)}, f32[768]{0:T(1024)}, u32[]{:S(2)}) copy-start(f32[768]{0:T(1024)} %copy-done.32) | copy-start | bytes 9220
  162.0 114.3 %copy-start.35 = (f32[768]{0:T(1024)S(1)}, f32[768]{0:T(1024)}, u32[]{:S(2)}) copy-start(f32[768]{0:T(1024)} %copy-done.34) | copy-start | bytes 9220
  162.0 114.3 %copy-start.37 = (f32[768]{0:T(1024)S(1)}, f32[768]{0:T(1024)}, u32[]{:S(2)}) copy-start(f32[768]{0:T(1024)} %copy-done.36) | copy-start | bytes 9220
  162.0 114.3 %copy-start.39 = (f32[768]{0:T(1024)S(1)}, f32[768]{0:T(1024)}, u32[]{:S(2)}) copy-start(f32[768]{0:T(1024)} %copy-done.38) | copy-start | bytes 9220
  162.0 114.3 %copy-start.41 = (f32[768]{0:T(1024)S(1)}, f32[768]{0:T(1024)}, u32[]{:S(2)}) copy-start(f32[768]{0:T(1024)} %copy-done.40) | copy-start | bytes 9220
  162.1 114.3 %copy-start.43 = (f32[768]{0:T(1024)S(1)}, f32[768]{0:T(1024)}, u32[]{:S(2)}) copy-start(f32[768]{0:T(1024)} %copy-done.42) | copy-start | bytes 9220
  162.1 114.3 %copy-start.45 = (f32[768]{0:T(1024)S(1)}, f32[768]{0:T(1024)}, u32[]{:S(2)}) copy-start(f32[768]{0:T(1024)} %copy-done.44) | copy-start | bytes 9220
  162.1 114.3 %copy-start.47 = (f32[768]{0:T(1024)S(1)}, f32[768]{0:T(1024)}, u32[]{:S(2)}) copy-start(f32[768]{0:T(1024)} %copy-done.46) | copy-start | bytes 9220
  162.1 114.3 %copy-start.49 = (f32[768]{0:T(1024)S(1)}, f32[768]{0:T(1024)}, u32[]{:S(2)}) copy-start(f32[768]{0:T(1024)} %copy-done.48) | copy-start | bytes 9220
  162.1 14.9 %collective-permute-start.4 = (bf16[3,64,768]{2,1,0:T(8,128)(2,1)S(1)}, bf16[3,64,768]{2,1,0:T(8,128)(2,1)S(1)}, u32[]{:S(2)}, u32[]{:S(2)}) collective-permute-start(bf16[3,64,768]{2,1,0:T(8,128)(2,1)S(1)} %get-tuple-element.113), channel_id=1, source_target_pairs={{0,2},{2,4},{4,6},{6,8},{8,10},{10,12},{12,14},{14,16},{16,18},{18... | collective-permute-start | bytes 884744 | tf_op jit(solution)/shard_map/ppermute | solution.py:17
  163.5 14.2 %collective-permute-start.5 = (bf16[3,64,768]{2,1,0:T(8,128)(2,1)S(1)}, bf16[3,64,768]{2,1,0:T(8,128)(2,1)S(1)}, u32[]{:S(2)}, u32[]{:S(2)}) collective-permute-start(bf16[3,64,768]{2,1,0:T(8,128)(2,1)S(1)} %get-tuple-element.114), channel_id=1, source_target_pairs={{2,0},{4,2},{6,4},{8,6},{10,8},{12,10},{14,12},{16,14},{18,16},{20... | collective-permute-start | bytes 884744 | tf_op jit(solution)/shard_map/ppermute | solution.py:19
  177.8 98.1 %collective-permute-start.6 = (bf16[10,3,768]{2,1,0:T(4,128)(2,1)S(1)}, bf16[10,3,768]{2,1,0:T(4,128)(2,1)S(1)}, u32[]{:S(2)}, u32[]{:S(2)}) collective-permute-start(bf16[10,3,768]{2,1,0:T(4,128)(2,1)S(1)} %get-tuple-element.109), channel_id=1, source_target_pairs={{0,1},{2,3},{4,5},{6,7},{8,9},{10,11},{12,13},{14,15},{16,17},{18,... | collective-permute-start | bytes 138248 | tf_op jit(solution)/shard_map/ppermute | solution.py:17
  179.8 96.1 %collective-permute-start.7 = (bf16[10,3,768]{2,1,0:T(4,128)(2,1)S(1)}, bf16[10,3,768]{2,1,0:T(4,128)(2,1)S(1)}, u32[]{:S(2)}, u32[]{:S(2)}) collective-permute-start(bf16[10,3,768]{2,1,0:T(4,128)(2,1)S(1)} %get-tuple-element.110), channel_id=1, source_target_pairs={{1,0},{3,2},{5,4},{7,6},{9,8},{11,10},{13,12},{15,14},{17,16},{19,... | collective-permute-start | bytes 138248 | tf_op jit(solution)/shard_map/ppermute | solution.py:19
  276.4 283.4 %copy-start.13 = (f32[49,768]{1,0:T(8,128)S(1)}, f32[49,768]{1,0:T(8,128)}, u32[]{:S(2)}) copy-start(f32[49,768]{1,0:T(8,128)} %get-tuple-element.127) | copy-start | bytes 451588
  (25 other events, 110.6 us)
Sparse Core Ops, SparseCore 0:
  150.2 124.2 all-reduce.4
  282.0 136.3 reduce-scatter.4
  424.8 134.8 reduce-scatter.2
where the time goes:
time: 568 us; the launch traced here: 567 us
  waiting for transfers between devices  383 us (67%)
  blocking collectives  84.6 us (15%)
  matrix products  27.3 us (5%)
  other arithmetic  25.6 us (5%)
  starting transfers between devices  16.7 us (3%)
  between operations  15.2 us (3%)
  local copies, waits for them, and re-layouts  14.9 us (3%)
    reduce_scatter x1, waiting for transfers between devices, shards(): lax.psum_scatter(full_in, ('row', 'col'), scatter_dimension=1, tiled=True)  141 us
    reduce_scatter x1, waiting for transfers between devices, shards(): lax.psum_scatter(full_out, ('row', 'col'), scatter_dimension=0, tiled=True)  135 us
    unnamed x4, waiting for transfers between devices  93.4 us
    unnamed x1, blocking collectives  44.4 us
    all_gather x1, blocking collectives, shards(): every_grad = lax.all_gather(region_grad, ('row', 'col'), axis=0, tiled=True)  40.2 us
    ppermute x4, waiting for transfers between devices, extended(): lax.ppermute(tail, axis, [(i, (i + 1) % count) for i in range(ends)])  11.6 us
  transfers between devices with their start and end apart: 11, of which 5 were waited for; matrix products, arithmetic and copies ran while one was open for 4% of the time, Pallas kernels for 0%

commit v1 on v0

v1 whole, which is shorter than its diff:
```python
import functools
import math

import jax
import jax.numpy as jnp
from jax import lax
from jax.experimental import pallas as pl
from jax.experimental.pallas import tpu as pltpu
from jax.sharding import PartitionSpec as P

MESH = pl.DeviceIdType.MESH
EDGE = 16


def log2(count):
    bits = count.bit_length() - 1
    assert 1 << bits == count
    return bits


def bit(value, k):
    return lax.rem(lax.div(value, 1 << k), 2)


def place(index):
    return {"row": lax.div(index, 2), "col": lax.rem(index, 2)}


class Halo:
    def __init__(self, src, up, down, side, send, recv, row, col, rows):
        self.has_up, self.has_down = row > 0, row < rows - 1
        h, w = src.shape[0], src.shape[1]
        above, below = jnp.maximum(row - 1, 0), jnp.minimum(row + 1, rows - 1)
        cols = pl.ds(pl.multiple_of((1 - col) * (w - EDGE), EDGE), EDGE)
        last, first = pl.ds(h - 3, 3), pl.ds(0, 3)

        def copy(k, s, d, r, c):
            return pltpu.make_async_remote_copy(
                src_ref=s, dst_ref=d, send_sem=send.at[k], recv_sem=recv.at[k],
                device_id={"row": r, "col": c}, device_id_type=MESH,
            )

        self.up, self.down, self.side = up, down, side
        self.to_down = [
            copy(0, src.at[last], up, below, col),
            copy(1, src.at[last, cols], side.at[pl.ds(0, 3)], below, 1 - col),
        ]
        self.to_up = [
            copy(2, src.at[first], down, above, col),
            copy(3, src.at[first, cols], side.at[pl.ds(h + 3, 3)], above, 1 - col),
        ]
        self.across = copy(4, src.at[:, cols], side.at[pl.ds(3, h)], row, 1 - col)
        self.h = h
        self.targets = (above, below, row, col)

    def greet(self, barrier):
        above, below, row, col = self.targets
        pl.semaphore_signal(barrier, inc=1, device_id={"row": row, "col": 1 - col}, device_id_type=MESH)

        @pl.when(self.has_up)
        def _():
            for c in (col, 1 - col):
                pl.semaphore_signal(barrier, inc=1, device_id={"row": above, "col": c}, device_id_type=MESH)

        @pl.when(self.has_down)
        def _():
            for c in (col, 1 - col):
                pl.semaphore_signal(barrier, inc=1, device_id={"row": below, "col": c}, device_id_type=MESH)

        return 1 + 2 * self.has_up.astype(jnp.int32) + 2 * self.has_down.astype(jnp.int32)

    def start(self):
        self.across.start()

        @pl.when(self.has_down)
        def _():
            for c in self.to_down:
                c.start()

        @pl.when(self.has_up)
        def _():
            for c in self.to_up:
                c.start()

        @pl.when(jnp.logical_not(self.has_up))
        def _():
            self.up[...] = jnp.zeros_like(self.up)
            self.side[0:3] = jnp.zeros((3,) + self.side.shape[1:], self.side.dtype)

        @pl.when(jnp.logical_not(self.has_down))
        def _():
            self.down[...] = jnp.zeros_like(self.down)
            self.side[self.h + 3 : self.h + 6] = jnp.zeros((3,) + self.side.shape[1:], self.side.dtype)

    def finish(self):
        self.across.wait_send()
        self.across.wait_recv()

        @pl.when(self.has_down)
        def _():
            for c in self.to_down:
                c.wait_send()
            for c in self.to_up:
                c.wait_recv()

        @pl.when(self.has_up)
        def _():
            for c in self.to_up:
                c.wait_send()
            for c in self.to_down:
                c.wait_recv()


def gather_step(buf, send, recv, me, k):
    size = 1 << k
    start = lax.div(me, size) * size
    other = me + size * (1 - 2 * bit(me, k))
    return pltpu.make_async_remote_copy(
        src_ref=buf.at[pl.ds(start, size)], dst_ref=buf.at[pl.ds(start, size)],
        send_sem=send.at[k], recv_sem=recv.at[k],
        device_id=place(other), device_id_type=MESH,
    )


def greet_partners(barrier, me, levels):
    for k in range(levels):
        other = me + (1 << k) * (1 - 2 * bit(me, k))
        pl.semaphore_signal(barrier, inc=1, device_id=place(other), device_id_type=MESH)
    return levels


def opening(rows, src, msg, up, down, side, every, hs, hr, gs, gr):
    row, col = lax.axis_index("row"), lax.axis_index("col")
    me = row * 2 + col
    levels = log2(rows * 2)
    halo = Halo(src, up, down, side, hs, hr, row, col, rows)
    barrier = pltpu.get_barrier_semaphore()
    amount = halo.greet(barrier) + greet_partners(barrier, me, levels)
    pl.semaphore_wait(barrier, amount)
    every[me] = msg[...]
    halo.start()
    for k in range(levels):
        step = gather_step(every, gs, gr, me, k)
        step.start()
        step.wait_send()
        step.wait_recv()
    halo.finish()


def closing(rows, kr, slots, wi, ht, ex, src, wi_out, ht_out, ex_out, every, up, down, side,
            wi_in, ht_in, ex_in, wi_acc, ht_acc, ex_acc, wi_buf, ht_buf, ex_buf,
            s0, r0, ss, rs, hs, hr, gs, gr):
    row, col = lax.axis_index("row"), lax.axis_index("col")
    me = row * 2 + col
    levels = log2(rows * 2)
    nb = levels - 1
    halo = Halo(src, up, down, side, hs, hr, row, col, rows)
    barrier = pltpu.get_barrier_semaphore()
    amount = halo.greet(barrier) + greet_partners(barrier, me, levels)
    pl.semaphore_wait(barrier, amount)

    def order(p):
        head = list(range(nb - 1))
        p = p % max(nb - 1, 1)
        return head[p:] + head[:p] + [nb - 1]

    third = wi.shape[3] // 3
    parts = [
        (ex, ex_in, ex_acc, ex_buf, ex_out, pl.ds(0, ex.shape[3]), order(2)),
        (wi, wi_in, wi_acc, wi_buf, wi_out, pl.ds(0, third), order(0)),
        (wi, wi_in, wi_acc, wi_buf, wi_out, pl.ds(third, third), order(1)),
        (wi, wi_in, wi_acc, wi_buf, wi_out, pl.ds(2 * third, third), order(2)),
        (ht, ht_in, ht_acc, ht_buf, ht_out, pl.ds(0, ht.shape[3]), order(0)),
    ]
    swaps = []
    for p, (full, landed, _, _, _, lanes, _) in enumerate(parts):
        swap = pltpu.make_async_remote_copy(
            src_ref=full.at[:, 1 - col, :, lanes], dst_ref=landed.at[:, :, lanes],
            send_sem=s0.at[p], recv_sem=r0.at[p],
            device_id={"row": row, "col": 1 - col}, device_id_type=MESH,
        )
        swap.start()
        swaps.append(swap)
    halo.start()
    mine = [bit(row, k) for k in range(nb)]

    def combos(bits):
        return [[(b, (j >> i) & 1) for i, b in enumerate(bits)] for j in range(1 << len(bits))]

    def step(p, s, free, make=True):
        _, _, acc, buf, _, lanes, bits = parts[p]
        b = bits[s]
        partner = row + (1 << b) * (1 - 2 * mine[b])
        away = (1 - mine[b]) * (1 << b)
        for done in bits[:s]:
            away = away + mine[done] * (1 << done)
        rest = bits[s + 1 :]
        value = dict(free)
        slot = (1 << nb) - (1 << (nb - s))
        for i, f in enumerate(rest):
            away = away + value[f] * (1 << f)
            slot = slot + value[f] * (1 << i)
        home = away + (2 * mine[b] - 1) * (1 << b)
        if not make:
            return None, home, slot
        copy = pltpu.make_async_remote_copy(
            src_ref=acc.at[away, :, lanes], dst_ref=buf.at[slot, :, lanes],
            send_sem=ss.at[p, slot], recv_sem=rs.at[p, slot],
            device_id={"row": partner, "col": col}, device_id_type=MESH,
        )
        return copy, home, slot

    for p, (full, landed, acc, _, _, lanes, bits) in enumerate(parts):
        swaps[p].wait_recv()
        for first in (1, 0):
            for free in combos(bits[1:]):
                copy, home, _ = step(p, 0, free, bool(first))
                b = bits[0]
                at = home - (2 * mine[b] - 1) * (1 << b) if first else home
                acc[at, :, lanes] = (
                    full[at, col, :, lanes].astype(jnp.float32) + landed[at, :, lanes].astype(jnp.float32)
                ).astype(acc.dtype)
                if first:
                    copy.start()
    for s in range(nb):
        for p, (_, _, acc, buf, out, lanes, bits) in enumerate(parts):
            rest = bits[s + 1 :]
            if not rest:
                copy, home, slot = step(p, s, [])
                copy.wait_recv()
                out[:, lanes] = acc[home, :, lanes].astype(jnp.float32) + buf[slot, :, lanes].astype(jnp.float32)
                continue
            b = rest[0]
            for first in (1, 0):
                for free in combos(rest[1:]):
                    now = free + [(b, 1 - mine[b] if first else mine[b])]
                    copy, home, slot = step(p, s, now)
                    copy.wait_recv()
                    acc[home, :, lanes] = (
                        acc[home, :, lanes].astype(jnp.float32) + buf[slot, :, lanes].astype(jnp.float32)
                    ).astype(acc.dtype)
                    if first:
                        onward, _, _ = step(p, s + 1, free)
                        onward.start()
    chunks = ex.shape[3] // 128
    own = [ex_out[slots : slots + kr, 128 * i : 128 * i + 128] for i in range(chunks)]
    pad = every.shape[1] - kr * chunks
    if pad:
        own.append(jnp.zeros((pad, 128), jnp.float32))
    every[me] = jnp.concatenate(own, axis=0)
    for k in range(levels):
        hop = gather_step(every, gs, gr, me, k)
        hop.start()
        hop.wait_send()
        hop.wait_recv()
    halo.finish()
    for p, (_, _, _, _, _, _, bits) in enumerate(parts):
        swaps[p].wait_send()
        for s in range(nb):
            for free in combos(bits[s + 1 :]):
                step(p, s, free)[0].wait_send()


def halo_shapes(h, w, c):
    return (
        jax.ShapeDtypeStruct((3, w, c), jnp.bfloat16),
        jax.ShapeDtypeStruct((3, w, c), jnp.bfloat16),
        jax.ShapeDtypeStruct((h + 6, EDGE, c), jnp.bfloat16),
    )


def joined(block, up, down, side, col):
    centre = jnp.concatenate([up, block, down], axis=0)
    zero = jnp.zeros_like(side[:, :3])
    left = jnp.where(col == 1, side[:, EDGE - 3 :], zero)
    right = jnp.where(col == 0, side[:, :3], zero)
    return jnp.concatenate([left, centre, right], axis=1)


def depthwise(padded, taps, height, breadth, flipped):
    total = jnp.zeros((height, breadth, padded.shape[2]), jnp.float32)
    for a in range(7):
        if flipped:
            terms = [
                padded[6 - a : 6 - a + height, 6 - b : 6 - b + breadth] * taps[a, b]
                for b in range(7)
            ]
        else:
            terms = [padded[a : a + height, b : b + breadth] * taps[a, b] for b in range(7)]
        row_total = terms[0]
        for term in terms[1:]:
            row_total = row_total + term
        total = total + row_total
    return total


VMEM = pl.BlockSpec(memory_space=pltpu.VMEM)
DMA = pltpu.SemaphoreType.DMA


def shards(image, dw_kernel, w_in, w_out, layer_scale, region_ids, region_slot, pool_grad):
    height, breadth, width = image.shape
    rows, cols = lax.axis_size("row"), lax.axis_size("col")
    assert cols == 2
    n = rows * cols
    levels = log2(n)
    row, col = lax.axis_index("row"), lax.axis_index("col")
    me = row * 2 + col
    taps = dw_kernel.reshape(7, 7, width)
    regions = region_slot.shape[0]
    slots = pool_grad.shape[0]
    hidden_width = w_in.shape[1]

    labels = region_ids.reshape(-1)
    region_iota = jnp.arange(regions, dtype=jnp.int32)
    id_onehot = (labels[:, None] == region_iota[None, :]).astype(jnp.bfloat16)
    slot_onehot = (region_slot[:, None] == region_iota[None, :]).astype(jnp.bfloat16)
    tile_onehot = jnp.dot(id_onehot, slot_onehot, preferred_element_type=jnp.float32)
    local_count = jnp.sum(tile_onehot, axis=0)
    payload = jnp.concatenate([pool_grad.reshape(-1), local_count.astype(jnp.bfloat16)])
    height16 = -(-payload.shape[0] // (256 * 16)) * 16
    message = jnp.pad(payload, (0, height16 * 256 - payload.shape[0])).reshape(height16, 256)

    up, down, side, every = pl.pallas_call(
        functools.partial(opening, rows),
        out_shape=halo_shapes(height, breadth, width)
        + (jax.ShapeDtypeStruct((n, height16, 256), jnp.bfloat16),),
        in_specs=[VMEM] * 2,
        out_specs=(VMEM,) * 4,
        scratch_shapes=[DMA((5,)), DMA((5,)), DMA((levels,)), DMA((levels,))],
        compiler_params=pltpu.CompilerParams(
            collective_id=0, has_side_effects=True, vmem_limit_bytes=16 << 20
        ),
        name="opening",
    )(image, message)
    flat = every.reshape(n, -1)
    every_pool = flat[:, : slots * width].reshape(regions, width)
    count = jnp.sum(flat[:, slots * width : slots * width + regions].astype(jnp.float32), axis=0)
    region_grad = (every_pool.astype(jnp.float32) / (4.0 * count)[:, None]).astype(jnp.bfloat16)

    pos_onehot = jnp.broadcast_to(
        tile_onehot.astype(jnp.bfloat16).reshape(height // 2, 1, breadth // 2, 1, regions),
        (height // 2, 2, breadth // 2, 2, regions),
    ).reshape(-1, regions)

    xfull = image.astype(jnp.float32)
    xpad = joined(image, up, down, side, col).astype(jnp.float32)
    conv = depthwise(xpad, taps, height, breadth, False)
    centre = conv - jnp.mean(conv, axis=-1, keepdims=True)
    inv_std = lax.rsqrt(jnp.mean(centre * centre, axis=-1, keepdims=True) + 1e-06)
    normed_f = centre * inv_std
    normed = normed_f.astype(jnp.bfloat16).reshape(-1, width)
    pre = jnp.dot(normed, w_in, preferred_element_type=jnp.float32)
    cdf = 0.5 * (1.0 + lax.erf(pre / math.sqrt(2.0)))
    hidden = (pre * cdf).astype(jnp.bfloat16)
    branch = jnp.dot(hidden, w_out, preferred_element_type=jnp.float32).reshape(
        height, breadth, width
    )
    block = (xfull + layer_scale * branch).astype(jnp.bfloat16).reshape(-1, width)
    first = (((0,), (0,)), ((), ()))
    partial_sum = lax.dot_general(pos_onehot, block, first, preferred_element_type=jnp.float32)

    dblock = jnp.dot(pos_onehot, region_grad, preferred_element_type=jnp.float32)
    g_out = (dblock * layer_scale).astype(jnp.bfloat16)
    dblock = dblock.reshape(height, breadth, width)
    dhidden = jnp.dot(g_out, w_out.T, preferred_element_type=jnp.float32)
    density = jnp.exp(-0.5 * pre * pre) / math.sqrt(2.0 * math.pi)
    g_in = (dhidden * (cdf + pre * density)).astype(jnp.bfloat16)
    part_in = lax.dot_general(g_in, normed, first, preferred_element_type=jnp.float32)
    part_hid = lax.dot_general(hidden, pos_onehot, first, preferred_element_type=jnp.float32)
    dnorm = jnp.dot(g_in, w_in.T, preferred_element_type=jnp.float32).reshape(
        height, breadth, width
    )
    dconv = inv_std * (
        dnorm
        - jnp.mean(dnorm, axis=-1, keepdims=True)
        - normed_f * jnp.mean(dnorm * normed_f, axis=-1, keepdims=True)
    )
    kernel_rows = []
    for a in range(7):
        for b in range(7):
            kernel_rows.append(jnp.sum(xpad[a : a + height, b : b + breadth] * dconv, axis=(0, 1)))
    kr = -(-49 // n)
    part_kernel = jnp.pad(jnp.stack(kernel_rows, axis=0), ((0, kr * n - 49), (0, 0)))

    depth = hidden_width // n
    wi = part_in.astype(jnp.bfloat16).reshape(rows, 2, depth, width)
    ht = part_hid.astype(jnp.bfloat16).reshape(rows, 2, depth, regions)
    tall = -(-(slots + kr) // 16) * 16
    ex = jnp.concatenate(
        [
            partial_sum.reshape(n, slots, width),
            part_kernel.reshape(n, kr, width),
            jnp.zeros((n, tall - slots - kr, width), jnp.float32),
        ],
        axis=1,
    ).astype(jnp.bfloat16).reshape(rows, 2, tall, width)
    dconv_b = dconv.astype(jnp.bfloat16)
    ktall = -(-(kr * width // 128) // 8) * 8
    f32 = jnp.float32
    b16 = jnp.bfloat16

    def three(lead):
        return [
            pltpu.VMEM((lead, depth, width), b16),
            pltpu.VMEM((lead, depth, regions), b16),
            pltpu.VMEM((lead, tall, width), b16),
        ]

    wi_sum, ht_sum, ex_sum, every_kernel, up, down, side = pl.pallas_call(
        functools.partial(closing, rows, kr, slots),
        out_shape=(
            jax.ShapeDtypeStruct((depth, width), f32),
            jax.ShapeDtypeStruct((depth, regions), f32),
            jax.ShapeDtypeStruct((tall, width), f32),
            jax.ShapeDtypeStruct((n, ktall, 128), f32),
        )
        + halo_shapes(height, breadth, width),
        in_specs=[VMEM] * 4,
        out_specs=(VMEM,) * 7,
        scratch_shapes=three(rows) + three(rows) + three(rows)
        + [DMA((5,)), DMA((5,)), DMA((5, rows)), DMA((5, rows)),
           DMA((5,)), DMA((5,)), DMA((levels,)), DMA((levels,))],
        compiler_params=pltpu.CompilerParams(
            collective_id=1, has_side_effects=True, vmem_limit_bytes=56 << 20
        ),
        name="closing",
    )(wi, ht, ex, dconv_b)

    own_count = lax.dynamic_slice_in_dim(count, me * slots, slots)
    region_pool = ex_sum[:slots] / (4.0 * own_count)[:, None]
    grad_w_in = wi_sum.T
    scaled = (region_grad.astype(f32) * layer_scale).astype(b16).astype(f32)
    grad_w_out = jnp.dot(ht_sum, scaled, precision=lax.Precision.HIGHEST, preferred_element_type=f32)
    chunks = width // 128
    grad_kernel = (
        every_kernel[:, : kr * chunks]
        .reshape(n, chunks, kr, 128)
        .transpose(0, 2, 1, 3)
        .reshape(n * kr, width)[:49]
    )
    dpad = joined(dconv_b, up, down, side, col).astype(f32)
    back = depthwise(dpad, taps, height, breadth, True)
    grad_image = (dblock + back).astype(b16)
    return (region_pool, grad_image, grad_w_in, grad_w_out, grad_kernel)


def solution(mesh):
    placed = (
        P(("slides", "row"), "col", None),
        P(),
        P(),
        P(),
        P(),
        P(("slides", "row"), "col"),
        P("slides"),
        P(("slides", "row", "col"), None),
    )
    return jax.shard_map(
        shards,
        mesh=mesh,
        in_specs=placed,
        out_specs=(
            P(("slides", "row", "col"), None),
            P(("slides", "row"), "col", None),
            P("slides", ("row", "col")),
            P(("slides", "row", "col"), None),
            P("slides", None),
        ),
        check_vma=False,
    )
```

time: 568 us -> 167 us (0.29)
  waiting for transfers between devices: 383 us -> 0 us
  Pallas kernels: 0 us -> 105 us
  blocking collectives: 84.6 us -> 0 us
  starting transfers between devices: 16.7 us -> 0 us
  between operations: 15.2 us -> 1.55 us
  local copies, waits for them, and re-layouts: 14.9 us -> 7.93 us
    reduce_scatter x2 -> x0, waiting for transfers between devices: 277 us -> none  [the longest x1 141 us: shards(): lax.psum_scatter(full_in, ('row', 'col'), scatter_dimension=1, tiled=True)]
    pallas_call x0 -> x2, Pallas kernels: none -> 105 us  [the longest x1 71.1 us: shards(): pl.pallas_call(functools.partial(closing, rows, kr, slots), out_shape=(ja...]
    unnamed x4 -> x0, waiting for transfers between devices: 93.4 us -> none
    unnamed x1 -> x0, blocking collectives: 44.4 us -> none
    all_gather x1 -> x0, blocking collectives: 40.2 us -> none  [shards(): every_grad = lax.all_gather(region_grad, ('row', 'col'), axis=0, tiled=True)]
    ppermute x8 -> x0, starting transfers between devices: 16.6 us -> none  [the longest x4 11.2 us: extended(): lax.ppermute(tail, axis, [(i, (i + 1) % count) for i in range(ends)])]
    ppermute x8 -> x0, waiting for transfers between devices: 12.3 us -> none  [the longest x4 11.6 us: extended(): lax.ppermute(tail, axis, [(i, (i + 1) % count) for i in range(ends)])]
    dot_general x4 -> x5, matrix products: 11.6 us -> 7.71 us  [the longest x1 3.65 us: shards(): lax.dot_general(g_in, normed, first, preferred_element_type=jnp.float32)]
  transfers between devices with their start and end apart: 11 -> 0, of which waited for: 5 -> 0; matrix products, arithmetic and copies ran while one was open for 4% -> 0% of each run, Pallas kernels for 0% -> 0%
where the time goes in v1:
time: 167 us
  Pallas kernels  105 us (63%)
  matrix products  27.1 us (16%)
  other arithmetic  25 us (15%)
  local copies, waits for them, and re-layouts  7.93 us (5%)
    pallas_call x1, Pallas kernels, shards(): pl.pallas_call(functools.partial(closing, rows, kr, slots), out_shape=(ja...  71.1 us
    pallas_call x1, Pallas kernels, shards(): pl.pallas_call(functools.partial(opening, rows), out_shape=halo_shapes(he...  33.9 us
    dot_general x1, matrix products, shards(): dhidden = jnp.dot(g_out, w_out.T, preferred_element_type=jnp.float32)  6.65 us
    convert_element_type x1, other arithmetic, shards(): grad_image = (dblock + back).astype(b16)  6.53 us
    dot_general x1, matrix products, shards(): pre = jnp.dot(normed, w_in, preferred_element_type=jnp.float32)  6.08 us
    reduce_sum x1, other arithmetic, shards(): centre = conv - jnp.mean(conv, axis=-1, keepdims=True)  6.04 us
    reduce_sum x3, other arithmetic, shards(): jnp.sum(xpad[a:a + height, b:b + breadth] * dconv, axis=(0, 1))  5 us
    dot_general x1, matrix products, shards(): jnp.dot(hidden, w_out, preferred_element_type=jnp.float32)  4.23 us

profile of v1, /device:TPU:0, one launch (start us, length us, event | category | flops | bytes accessed | tf_op | source)
XLA Modules:
  0.0 166.7 jit_solution(16787355311567345949)
XLA Ops:
  0.6 0.8 eq.36
  1.4 0.9 fusion.69
  2.3 0.7 reshape.110
  3.0 1.0 copy-done
  4.0 33.9 %opening.1 = (bf16[3,64,768]{2,1,0:T(8,128)(2,1)S(1)}, bf16[3,64,768]{2,1,0:T(8,128)(2,1)S(1)}, bf16[10,16,768]{2,1,0:T(8,128)(2,1)S(1)}, bf16[32,16,256]{2,1,0:T(8,128)(2,1)S(1)}) custom-call(bf16[4,64,768]{2,1,0:T(8,128)(2,1)S(1)} %copy-done, bf16[16,256]{1,0:T(8,128)(2,1)S(1)} %reshape.111.msg), custom_call_target="tpu_custom_call" | custom-call | tf_op jit(solution)/shard_map/opening/pallas_call | solution.py:324
  38.0 1.3 maximum_convert_fusion
  39.3 0.2 slice_reduce_fusion.47
  39.5 0.2 slice_reduce_fusion.48
  39.7 0.1 slice_reduce_fusion.46
  39.8 6.0 %fusion.68 = (f32[4,64]{1,0:T(4,128)S(1)}, f32[4,64,768]{2,1,0:T(8,128)S(1)}) fusion(f32[768]{0:T(1024)S(1)} %get-tuple-element.77, f32[10,70,768]{2,1,0:T(8,128)S(1)} %maximum_convert_fusion, f32[768]{0:T(1024)S(1)} %get-tuple-element.78, f32[768]{0:T(1024)S(1)} %get-tuple-element.79, f32[768]{0:T(1024)S(1)} %get-tuple-element.80, ...), kind=kLoop, calls=%fused_computation.252 | loop fusion | flops 19267328 | bytes 39473152 | tf_op jit(solution)/shard_map/reduce_sum | solution.py:349
  45.8 0.2 multiply_reduce_fusion.50
  46.1 0.2 fusion.55
  46.3 6.1 %multiply_convert_fusion = (bf16[256,3072]{1,0:T(8,128)(2,1)}, f32[256,3072]{1,0:T(8,128)}) fusion(bf16[256,768]{1,0:T(8,128)(2,1)S(1)} %bitcast.54, bf16[768,3072]{1,0:T(8,128)(2,1)} %param.10), kind=kOutput, calls=%fused_computation.9 | convolution fusion | flops 1211891712 | bytes 9830400 | tf_op jit(solution)/shard_map/dot_general | solution.py:353
  52.3 0.1 copy.26
  52.5 0.5 copy-done.20
  53.0 0.1 mul.1032
  53.1 0.1 div.49
  53.3 0.2 copy-done.22
  53.6 0.1 convert_element_type.82
  53.8 0.2 fusion.71
  54.0 6.7 %fusion = bf16[256,3072]{1,0:T(8,128)(2,1)S(1)} fusion(bf16[3072,768]{1,0:T(8,128)(2,1)} %param.11, f32[256,3072]{1,0:T(8,128)} %get-tuple-element.137, f32[256,768]{1,0:T(8,128)S(1)} %fusion.71, f32[768]{0:T(1024)S(1)} %copy-done.19), kind=kOutput, calls=%fused_computation.3 | convolution fusion | flops 1216217088 | bytes 10226688 | tf_op jit(solution)/shard_map/dot_general | solution.py:366
  60.7 1.5 fusion.70
  62.3 0.9 copy-done.7
  63.1 0.2 multiply_reduce_fusion.49
  63.4 0.1 div.59
  63.5 2.1 %fusion.67 = (bf16[4,64,768]{2,1,0:T(8,128)(2,1)}, f32[4,64,768]{2,1,0:T(8,128)S(1)}) fusion(f32[4,64]{1,0:T(4,128)S(1)} %broadcast_multiply_fusion, f32[4,64,768]{2,1,0:T(8,128)S(1)} %copy-done.3, f32[4,64]{1,0:T(4,128)S(1)} %broadcast_multiply_fusion.1, f32[4,64]{1,0:T(4,128)S(1)} %div.59, f32[256,768]{1,0:T(8,128)} %copy-done.7, ...), kind=kLoop, calls=%fused_computation.251 | loop fusion | flops 1376256 | bytes 2756608 | tf_op jit(solution)/shard_map/convert_element_type | solution.py:398
  65.6 1.9 %multiply_reduce_fusion = (bf16[768]{0:T(1024)(128)(2,1)S(1)}, bf16[768]{0:T(1024)(128)(2,1)S(1)}, bf16[768]{0:T(1024)(128)(2,1)S(1)}, bf16[768]{0:T(1024)(128)(...) fusion(f32[4,64,768]{2,1,0:T(8,128)S(1)} %get-tuple-element.126, ...), kind=kLoop, calls=%fused_computation.113 | loop fusion | flops 7064064 | bytes 14969856 | tf_op jit(solution)/shard_map/reduce_sum | solution.py:382
  67.7 2.0 %multiply_reduce_fusion.18 = (bf16[768]{0:T(1024)(128)(2,1)S(1)}, bf16[768]{0:T(1024)(128)(2,1)S(1)}, bf16[768]{0:T(1024)(128)(2,1)S(1)}, bf16[768]{0:T(1024)(12...) fusion(f32[4,64,768]{2,1,0:T(8,128)S(1)} %get-tuple-element.126, ...), kind=kLoop, calls=%fused_computation.131 | loop fusion | flops 7064064 | bytes 14969856 | tf_op jit(solution)/shard_map/reduce_sum | solution.py:382
  70.0 1.1 multiply_reduce_fusion.36
  71.3 0.4 stack.249
  71.7 4.2 %fusion.72 = f32[256,768]{1,0:T(8,128)S(1)} fusion(bf16[256,3072]{1,0:T(8,128)(2,1)} %get-tuple-element.136, bf16[3072,768]{1,0:T(8,128)(2,1)} %param.11), kind=kOutput, calls=%fused_computation.256 | convolution fusion | flops 1207959552 | bytes 7077888 | tf_op jit(solution)/shard_map/dot_general | solution.py:356
  76.0 0.1 add_convert_fusion
  76.1 0.1 copy.20
  76.2 0.2 fusion.59
  76.4 0.1 copy.33
  76.6 0.1 pad.18.clone
  76.6 1.3 maximum_maximum_fusion.ex
  77.9 3.6 %convolution_convert_fusion = bf16[3072,768]{1,0:T(8,128)(2,1)} fusion(bf16[256,3072]{1,0:T(8,128)(2,1)S(1)} %copy-done.6, bf16[256,768]{1,0:T(8,128)(2,1)S(1)} %bitcast.55), kind=kOutput, calls=%fused_computation | convolution fusion | flops 1210318848 | bytes 6684672 | tf_op jit(solution)/shard_map/dot_general | solution.py:369
  81.6 1.6 convolution_convert_fusion.1
  83.2 71.1 %closing.1 = (f32[96,768]{1,0:T(8,128)}, f32[96,128]{1,0:T(8,128)}, f32[16,768]{1,0:T(8,128)}, f32[32,16,128]{2,1,0:T(8,128)}, bf16[3,64,768]{2,1,0:T(8,128)(2,1...) custom-call(bf16[16,2,96,768]{3,2,1,0:T(8,128)(2,1)} %bitcast.47, bf16[16,2,96,128]{3,2,1,0:T(8,128)(2,1)} %bitcast.48, ...), custom_call_target="tpu_custom_call" | custom-call | tf_op jit(solution)/shard_map/closing/pallas_call | solution.py:410
  154.4 0.1 reshape.123
  154.5 2.0 %fusion.57 = f32[96,768]{1,0:T(8,128)} fusion(f32[96,128]{1,0:T(8,128)} %get-tuple-element.25, f32[768]{0:T(1024)S(1)} %copy-done.19, f32[128,768]{1,0:T(8,128)S(1)} %reshape.123, f32[128]{0:T(128)S(1)} %copy-done.23), kind=kOutput, calls=%fused_computation.175 | convolution fusion | flops 113737728 | bytes 740864 | tf_op jit(solution)/shard_map/dot_general | solution.py:434
  156.7 0.3 maximum_convert_fusion.1
  157.0 6.5 %fusion.8 = bf16[4,64,768]{2,1,0:T(8,128)(2,1)} fusion(f32[4,64,768]{2,1,0:T(8,128)S(1)} %bitcast.50, f32[10,70,768]{2,1,0:T(8,128)S(1)} %maximum_convert_fusion.1, f32[768]{0:T(1024)S(1)} %get-tuple-element.77, f32[768]{0:T(1024)S(1)} %get-tuple-element.78, f32[768]{0:T(1024)S(1)} %get-tuple-element.79, f32[768]{0:T(1024)S(1)} %get-tuple-element.80, ...), kind=kLoop, calls=%fused_computation.17 | loop fusion | flops 19464192 | bytes 39865344 | tf_op jit(solution)/shard_map/convert_element_type | solution.py:444
  163.6 0.1 copy.24
  163.8 0.7 slice.871
  164.5 1.4 slice_divide_fusion
  165.9 0.7 copy.36
  (120 shorter events, 1.1 us)
Async XLA Ops:
  3.0 1.0 copy-start
  4.0 35.3 %copy-start.17 = (f32[49,768]{1,0:T(8,128)S(1)}, f32[49,768]{1,0:T(8,128)}, u32[]{:S(2)}) copy-start(f32[49,768]{1,0:T(8,128)} %param.9) | copy-start | bytes 451588
  45.8 6.5 %copy-start.2 = (f32[4,64,768]{2,1,0:T(8,128)}, f32[4,64,768]{2,1,0:T(8,128)S(1)}, u32[]{:S(2)}) copy-start(f32[4,64,768]{2,1,0:T(8,128)S(1)} %get-tuple-element.128) | copy-start | bytes 2359300
  46.2 6.1 %copy-start.10 = (bf16[4,64,768]{2,1,0:T(8,128)(2,1)}, bf16[4,64,768]{2,1,0:T(8,128)(2,1)S(1)}, u32[]{:S(2)}) copy-start(bf16[4,64,768]{2,1,0:T(8,128)(2,1)S(1)} %fusion.55) | copy-start | bytes 1179652
  52.3 1.7 copy-start.19
  52.5 0.5 copy-start.20
  53.0 0.5 copy-start.22
  53.7 7.0 %slice-start = ((s8[4718592]{0:T(1024)(128)(4,1)}), s8[4194304]{0:T(1024)(128)(4,1)S(1)}, s32[]{:S(2)}) async-start(s8[4718592]{0:T(1024)(128)(4,1)} %bitcast.69), calls=%async_computation | async-start | bytes 8388608
  54.0 6.7 %copy-start.8 = (f32[256,768]{1,0:T(8,128)}, f32[256,768]{1,0:T(8,128)S(1)}, u32[]{:S(2)}) copy-start(f32[256,768]{1,0:T(8,128)S(1)} %fusion.71) | copy-start | bytes 2359300
  54.0 6.7 %slice-start.1 = ((s8[4718592]{0:T(1024)(128)(4,1)}), s8[524288]{0:T(1024)(128)(4,1)S(1)}, s32[]{:S(2)}) async-start(s8[4718592]{0:T(1024)(128)(4,1)} %bitcast.69), calls=%async_computation.1 | async-start | bytes 1048576
  60.7 1.5 copy-start.5
  60.7 2.4 %copy-start.3 = (f32[4,64,768]{2,1,0:T(8,128)S(1)}, f32[4,64,768]{2,1,0:T(8,128)}, u32[]{:S(2)}) copy-start(f32[4,64,768]{2,1,0:T(8,128)} %copy-done.2) | copy-start | bytes 2359300
  62.3 0.9 copy-start.7
  71.7 4.3 %copy-start.1 = (bf16[4,64,768]{2,1,0:T(8,128)(2,1)S(1)}, bf16[4,64,768]{2,1,0:T(8,128)(2,1)}, u32[]{:S(2)}) copy-start(bf16[4,64,768]{2,1,0:T(8,128)(2,1)} %src.1) | copy-start | bytes 1179652
  76.0 2.0 %copy-start.6 = (bf16[256,3072]{1,0:T(8,128)(2,1)S(1)}, bf16[256,3072]{1,0:T(8,128)(2,1)}, u32[]{:S(2)}) copy-start(bf16[256,3072]{1,0:T(8,128)(2,1)} %copy-done.5) | copy-start | bytes 4718596
  76.0 2.0 %copy-start.11 = (bf16[4,64,768]{2,1,0:T(8,128)(2,1)S(1)}, bf16[4,64,768]{2,1,0:T(8,128)(2,1)}, u32[]{:S(2)}) copy-start(bf16[4,64,768]{2,1,0:T(8,128)(2,1)} %copy-done.10) | copy-start | bytes 1179652
  77.9 3.7 %copy-start.12 = (bf16[256,3072]{1,0:T(8,128)(2,1)S(1)}, bf16[256,3072]{1,0:T(8,128)(2,1)}, u32[]{:S(2)}) copy-start(bf16[256,3072]{1,0:T(8,128)(2,1)} %get-tuple-element.136) | copy-start | bytes 4718596
  83.2 71.3 %copy-start.23 = (f32[128]{0:T(128)S(1)}, f32[128]{0:T(128)}, u32[]{:S(2)}) copy-start(f32[128]{0:T(128)} %copy-done.22) | copy-start | bytes 1540
  154.3 2.2 %copy-start.18 = (bf16[10,16,768]{2,1,0:T(8,128)(2,1)S(1)}, bf16[10,16,768]{2,1,0:T(8,128)(2,1)}, u32[]{:S(2)}) copy-start(bf16[10,16,768]{2,1,0:T(8,128)(2,1)} %get-tuple-element.21) | copy-start | bytes 737284
  154.3 2.3 %copy-start.4 = (bf16[4,64,768]{2,1,0:T(8,128)(2,1)S(1)}, bf16[4,64,768]{2,1,0:T(8,128)(2,1)}, u32[]{:S(2)}) copy-start(bf16[4,64,768]{2,1,0:T(8,128)(2,1)} %get-tuple-element.125.src) | copy-start | bytes 1179652
  154.3 2.3 %copy-start.13 = (bf16[3,64,768]{2,1,0:T(8,128)(2,1)S(1)}, bf16[3,64,768]{2,1,0:T(8,128)(2,1)}, u32[]{:S(2)}) copy-start(bf16[3,64,768]{2,1,0:T(8,128)(2,1)} %get-tuple-element.22) | copy-start | bytes 884740
  154.4 2.3 %copy-start.14 = (bf16[3,64,768]{2,1,0:T(8,128)(2,1)S(1)}, bf16[3,64,768]{2,1,0:T(8,128)(2,1)}, u32[]{:S(2)}) copy-start(bf16[3,64,768]{2,1,0:T(8,128)(2,1)} %get-tuple-element.23) | copy-start | bytes 884740
  154.5 2.4 %copy-start.9 = (f32[256,768]{1,0:T(8,128)S(1)}, f32[256,768]{1,0:T(8,128)}, u32[]{:S(2)}) copy-start(f32[256,768]{1,0:T(8,128)} %copy-done.8) | copy-start | bytes 2359300
  157.0 6.6 %copy-start.16 = (f32[32,16,128]{2,1,0:T(8,128)S(1)}, f32[32,16,128]{2,1,0:T(8,128)}, u32[]{:S(2)}) copy-start(f32[32,16,128]{2,1,0:T(8,128)} %get-tuple-element.26) | copy-start | bytes 786436
  157.0 7.5 %copy-start.21 = (f32[128]{0:T(128)S(1)}, f32[128]{0:T(128)}, u32[]{:S(2)}) copy-start(f32[128]{0:T(128)} %copy-done.20) | copy-start | bytes 1540
  157.0 9.0 %copy-start.15 = (f32[96,768]{1,0:T(8,128)S(1)}, f32[96,768]{1,0:T(8,128)}, u32[]{:S(2)}) copy-start(f32[96,768]{1,0:T(8,128)} %get-tuple-element.24) | copy-start | bytes 884740

commit v2 on v1

--- a/solution.py
+++ b/solution.py
@@ -20,10 +20,6 @@
 
 def bit(value, k):
     return lax.rem(lax.div(value, 1 << k), 2)
-
-
-def place(index):
-    return {"row": lax.div(index, 2), "col": lax.rem(index, 2)}
 
 
 class Halo:
@@ -111,77 +107,90 @@
                 c.wait_recv()
 
 
-def gather_step(buf, send, recv, me, k):
-    size = 1 << k
-    start = lax.div(me, size) * size
-    other = me + size * (1 - 2 * bit(me, k))
+def hop(src, dst, send, recv, row, col):
     return pltpu.make_async_remote_copy(
-        src_ref=buf.at[pl.ds(start, size)], dst_ref=buf.at[pl.ds(start, size)],
-        send_sem=send.at[k], recv_sem=recv.at[k],
-        device_id=place(other), device_id_type=MESH,
-    )
-
-
-def greet_partners(barrier, me, levels):
-    for k in range(levels):
-        other = me + (1 << k) * (1 - 2 * bit(me, k))
-        pl.semaphore_signal(barrier, inc=1, device_id=place(other), device_id_type=MESH)
-    return levels
+        src_ref=src, dst_ref=dst, send_sem=send, recv_sem=recv,
+        device_id={"row": row, "col": col}, device_id_type=MESH,
+    )
+
+
+def ahead(row, offset, rows):
+    return lax.rem(row + offset, rows)
+
+
+def greet_rows(barrier, row, col, rows):
+    for o in range(1, rows):
+        pl.semaphore_signal(
+            barrier, inc=1, device_id={"row": ahead(row, o, rows), "col": col}, device_id_type=MESH
+        )
+    return rows - 1
+
+
+def spread(buf, row, col, rows, send, recv):
+    own = buf.at[row, col]
+    return [
+        hop(own, own, send.at[o], recv.at[o], ahead(row, o, rows), col) for o in range(1, rows)
+    ]
+
+
+def share(buf, row, col, send, recv):
+    half = buf.at[:, col]
+    return hop(half, half, send.at[0], recv.at[0], row, 1 - col)
 
 
 def opening(rows, src, msg, up, down, side, every, hs, hr, gs, gr):
     row, col = lax.axis_index("row"), lax.axis_index("col")
-    me = row * 2 + col
-    levels = log2(rows * 2)
     halo = Halo(src, up, down, side, hs, hr, row, col, rows)
     barrier = pltpu.get_barrier_semaphore()
-    amount = halo.greet(barrier) + greet_partners(barrier, me, levels)
+    amount = halo.greet(barrier) + greet_rows(barrier, row, col, rows)
+    every[row, col] = msg[...]
     pl.semaphore_wait(barrier, amount)
-    every[me] = msg[...]
+    copies = spread(every, row, col, rows, gs, gr)
+    for copy in copies:
+        copy.start()
     halo.start()
-    for k in range(levels):
-        step = gather_step(every, gs, gr, me, k)
-        step.start()
-        step.wait_send()
-        step.wait_recv()
+    for copy in copies:
+        copy.wait_recv()
+    last = share(every, row, col, gs, gr)
+    last.start()
     halo.finish()
-
-
-def closing(rows, kr, slots, wi, ht, ex, src, wi_out, ht_out, ex_out, every, up, down, side,
+    last.wait_recv()
+    for copy in copies + [last]:
+        copy.wait_send()
+
+
+def closing(rows, skip, wi, ht, ex, src, wi_out, ht_out, ex_out, every, up, down, side,
             wi_in, ht_in, ex_in, wi_acc, ht_acc, ex_acc, wi_buf, ht_buf, ex_buf,
-            s0, r0, ss, rs, hs, hr, gs, gr):
+            s0, r0, ss, rs, hs, hr, es, er, gs, gr):
     row, col = lax.axis_index("row"), lax.axis_index("col")
-    me = row * 2 + col
-    levels = log2(rows * 2)
-    nb = levels - 1
+    nb = log2(rows)
+    f32 = jnp.float32
     halo = Halo(src, up, down, side, hs, hr, row, col, rows)
     barrier = pltpu.get_barrier_semaphore()
-    amount = halo.greet(barrier) + greet_partners(barrier, me, levels)
+    amount = halo.greet(barrier) + greet_rows(barrier, row, col, rows)
     pl.semaphore_wait(barrier, amount)
 
     def order(p):
         head = list(range(nb - 1))
-        p = p % max(nb - 1, 1)
-        return head[p:] + head[:p] + [nb - 1]
+        head = head[::-1] if p < 0 else head[p:] + head[:p]
+        return head + [nb - 1]
 
     third = wi.shape[3] // 3
     parts = [
-        (ex, ex_in, ex_acc, ex_buf, ex_out, pl.ds(0, ex.shape[3]), order(2)),
-        (wi, wi_in, wi_acc, wi_buf, wi_out, pl.ds(0, third), order(0)),
+        (wi, wi_in, wi_acc, wi_buf, wi_out, pl.ds(0, third), order(2)),
         (wi, wi_in, wi_acc, wi_buf, wi_out, pl.ds(third, third), order(1)),
-        (wi, wi_in, wi_acc, wi_buf, wi_out, pl.ds(2 * third, third), order(2)),
+        (wi, wi_in, wi_acc, wi_buf, wi_out, pl.ds(2 * third, third), order(-1)),
         (ht, ht_in, ht_acc, ht_buf, ht_out, pl.ds(0, ht.shape[3]), order(0)),
     ]
+    extra = hop(ex.at[:, 1 - col], ex_in, s0.at[len(parts)], r0.at[len(parts)], row, 1 - col)
+    extra.start()
     swaps = []
     for p, (full, landed, _, _, _, lanes, _) in enumerate(parts):
-        swap = pltpu.make_async_remote_copy(
-            src_ref=full.at[:, 1 - col, :, lanes], dst_ref=landed.at[:, :, lanes],
-            send_sem=s0.at[p], recv_sem=r0.at[p],
-            device_id={"row": row, "col": 1 - col}, device_id_type=MESH,
+        swap = hop(
+            full.at[:, 1 - col, :, lanes], landed.at[:, :, lanes], s0.at[p], r0.at[p], row, 1 - col
         )
         swap.start()
         swaps.append(swap)
-    halo.start()
     mine = [bit(row, k) for k in range(nb)]
 
     def combos(bits):
@@ -203,10 +212,9 @@
         home = away + (2 * mine[b] - 1) * (1 << b)
         if not make:
             return None, home, slot
-        copy = pltpu.make_async_remote_copy(
-            src_ref=acc.at[away, :, lanes], dst_ref=buf.at[slot, :, lanes],
-            send_sem=ss.at[p, slot], recv_sem=rs.at[p, slot],
-            device_id={"row": partner, "col": col}, device_id_type=MESH,
+        copy = hop(
+            acc.at[away, :, lanes], buf.at[slot, :, lanes], ss.at[p, slot], rs.at[p, slot],
+            partner, col,
         )
         return copy, home, slot
 
@@ -218,17 +226,30 @@
                 b = bits[0]
                 at = home - (2 * mine[b] - 1) * (1 << b) if first else home
                 acc[at, :, lanes] = (
-                    full[at, col, :, lanes].astype(jnp.float32) + landed[at, :, lanes].astype(jnp.float32)
+                    full[at, col, :, lanes].astype(f32) + landed[at, :, lanes].astype(f32)
                 ).astype(acc.dtype)
                 if first:
                     copy.start()
+        if p == 0:
+            extra.wait_recv()
+            for r in range(rows):
+                ex_acc[r] = (ex[r, col].astype(f32) + ex_in[r].astype(f32)).astype(ex_acc.dtype)
+            tosses = []
+            for o in range(1, rows):
+                to = ahead(row, o, rows)
+                toss = hop(ex_acc.at[to], ex_buf.at[o], es.at[o], er.at[o], to, col)
+                toss.start()
+                tosses.append(toss)
+            halo.start()
+    copies = spread(every, row, col, rows, gs, gr)
+    last = share(every, row, col, gs, gr)
     for s in range(nb):
         for p, (_, _, acc, buf, out, lanes, bits) in enumerate(parts):
             rest = bits[s + 1 :]
             if not rest:
                 copy, home, slot = step(p, s, [])
                 copy.wait_recv()
-                out[:, lanes] = acc[home, :, lanes].astype(jnp.float32) + buf[slot, :, lanes].astype(jnp.float32)
+                out[:, lanes] = acc[home, :, lanes].astype(f32) + buf[slot, :, lanes].astype(f32)
                 continue
             b = rest[0]
             for first in (1, 0):
@@ -237,23 +258,28 @@
                     copy, home, slot = step(p, s, now)
                     copy.wait_recv()
                     acc[home, :, lanes] = (
-                        acc[home, :, lanes].astype(jnp.float32) + buf[slot, :, lanes].astype(jnp.float32)
+                        acc[home, :, lanes].astype(f32) + buf[slot, :, lanes].astype(f32)
                     ).astype(acc.dtype)
                     if first:
                         onward, _, _ = step(p, s + 1, free)
                         onward.start()
-    chunks = ex.shape[3] // 128
-    own = [ex_out[slots : slots + kr, 128 * i : 128 * i + 128] for i in range(chunks)]
-    pad = every.shape[1] - kr * chunks
-    if pad:
-        own.append(jnp.zeros((pad, 128), jnp.float32))
-    every[me] = jnp.concatenate(own, axis=0)
-    for k in range(levels):
-        hop = gather_step(every, gs, gr, me, k)
-        hop.start()
-        hop.wait_send()
-        hop.wait_recv()
+        if s == 0:
+            total = ex_acc[row].astype(f32)
+            for o in range(1, rows):
+                tosses[o - 1].wait_recv()
+                total = total + ex_buf[o].astype(f32)
+            ex_out[...] = total
+            every[row, col] = total[skip : skip + every.shape[2]]
+            for copy in copies:
+                copy.start()
+        if s == nb - 2:
+            for copy in copies:
+                copy.wait_recv()
+            last.start()
     halo.finish()
+    last.wait_recv()
+    for copy in copies + tosses + [last, extra]:
+        copy.wait_send()
     for p, (_, _, _, _, _, _, bits) in enumerate(parts):
         swaps[p].wait_send()
         for s in range(nb):
@@ -303,7 +329,6 @@
     rows, cols = lax.axis_size("row"), lax.axis_size("col")
     assert cols == 2
     n = rows * cols
-    levels = log2(n)
     row, col = lax.axis_index("row"), lax.axis_index("col")
     me = row * 2 + col
     taps = dw_kernel.reshape(7, 7, width)
@@ -324,10 +349,10 @@
     up, down, side, every = pl.pallas_call(
         functools.partial(opening, rows),
         out_shape=halo_shapes(height, breadth, width)
-        + (jax.ShapeDtypeStruct((n, height16, 256), jnp.bfloat16),),
+        + (jax.ShapeDtypeStruct((rows, 2, height16, 256), jnp.bfloat16),),
         in_specs=[VMEM] * 2,
         out_specs=(VMEM,) * 4,
-        scratch_shapes=[DMA((5,)), DMA((5,)), DMA((levels,)), DMA((levels,))],
+        scratch_shapes=[DMA((5,)), DMA((5,)), DMA((rows,)), DMA((rows,))],
         compiler_params=pltpu.CompilerParams(
             collective_id=0, has_side_effects=True, vmem_limit_bytes=16 << 20
         ),
@@ -386,17 +411,19 @@
     depth = hidden_width // n
     wi = part_in.astype(jnp.bfloat16).reshape(rows, 2, depth, width)
     ht = part_hid.astype(jnp.bfloat16).reshape(rows, 2, depth, regions)
-    tall = -(-(slots + kr) // 16) * 16
+    lanes = 384
+    skip, keep = slots * width // lanes, kr * width // lanes
+    tall = -(-(skip + 8) // 16) * 16
+    assert width % lanes == 0 and skip % 8 == 0 and keep <= 8
     ex = jnp.concatenate(
         [
-            partial_sum.reshape(n, slots, width),
-            part_kernel.reshape(n, kr, width),
-            jnp.zeros((n, tall - slots - kr, width), jnp.float32),
+            partial_sum.reshape(n, skip, lanes),
+            part_kernel.reshape(n, keep, lanes),
+            jnp.zeros((n, tall - skip - keep, lanes), jnp.float32),
         ],
         axis=1,
-    ).astype(jnp.bfloat16).reshape(rows, 2, tall, width)
+    ).astype(jnp.bfloat16).reshape(rows, 2, tall, lanes)
     dconv_b = dconv.astype(jnp.bfloat16)
-    ktall = -(-(kr * width // 128) // 8) * 8
     f32 = jnp.float32
     b16 = jnp.bfloat16
 
@@ -404,23 +431,23 @@
         return [
             pltpu.VMEM((lead, depth, width), b16),
             pltpu.VMEM((lead, depth, regions), b16),
-            pltpu.VMEM((lead, tall, width), b16),
+            pltpu.VMEM((lead, tall, lanes), b16),
         ]
 
     wi_sum, ht_sum, ex_sum, every_kernel, up, down, side = pl.pallas_call(
-        functools.partial(closing, rows, kr, slots),
+        functools.partial(closing, rows, skip),
         out_shape=(
             jax.ShapeDtypeStruct((depth, width), f32),
             jax.ShapeDtypeStruct((depth, regions), f32),
-            jax.ShapeDtypeStruct((tall, width), f32),
-            jax.ShapeDtypeStruct((n, ktall, 128), f32),
+            jax.ShapeDtypeStruct((tall, lanes), f32),
+            jax.ShapeDtypeStruct((rows, 2, 8, lanes), f32),
         )
         + halo_shapes(height, breadth, width),
         in_specs=[VMEM] * 4,
         out_specs=(VMEM,) * 7,
         scratch_shapes=three(rows) + three(rows) + three(rows)
-        + [DMA((5,)), DMA((5,)), DMA((5, rows)), DMA((5, rows)),
-           DMA((5,)), DMA((5,)), DMA((levels,)), DMA((levels,))],
+        + [DMA((5,)), DMA((5,)), DMA((4, rows)), DMA((4, rows)), DMA((5,)), DMA((5,)),
+           DMA((rows,)), DMA((rows,)), DMA((rows,)), DMA((rows,))],
         compiler_params=pltpu.CompilerParams(
             collective_id=1, has_side_effects=True, vmem_limit_bytes=56 << 20
         ),
@@ -428,17 +455,11 @@
     )(wi, ht, ex, dconv_b)
 
     own_count = lax.dynamic_slice_in_dim(count, me * slots, slots)
-    region_pool = ex_sum[:slots] / (4.0 * own_count)[:, None]
+    region_pool = ex_sum[:skip].reshape(slots, width) / (4.0 * own_count)[:, None]
     grad_w_in = wi_sum.T
     scaled = (region_grad.astype(f32) * layer_scale).astype(b16).astype(f32)
     grad_w_out = jnp.dot(ht_sum, scaled, precision=lax.Precision.HIGHEST, preferred_element_type=f32)
-    chunks = width // 128
-    grad_kernel = (
-        every_kernel[:, : kr * chunks]
-        .reshape(n, chunks, kr, 128)
-        .transpose(0, 2, 1, 3)
-        .reshape(n * kr, width)[:49]
-    )
+    grad_kernel = every_kernel[:, :, :keep].reshape(n * kr, width)[:49]
     dpad = joined(dconv_b, up, down, side, col).astype(f32)
     back = depthwise(dpad, taps, height, breadth, True)
     grad_image = (dblock + back).astype(b16)

time: 167 us -> 143 us (0.86)
  Pallas kernels: 105 us -> 80.9 us
    pallas_call x1, Pallas kernels: 71.1 us -> 55.9 us  [shards(): pl.pallas_call(functools.partial(closing, rows, skip), out_shape=(jax.Sha...]
    pallas_call x1, Pallas kernels: 33.9 us -> 25 us  [shards(): pl.pallas_call(functools.partial(opening, rows), out_shape=halo_shapes(he...]
    unnamed x56 -> x103, local copies, waits for them, and re-layouts: 3.58 us -> 2.19 us
where the time goes in v2:
time: 143 us
  Pallas kernels  80.9 us (57%)
  matrix products  28.3 us (20%)
  other arithmetic  25.1 us (18%)
  local copies, waits for them, and re-layouts  6.35 us (4%)
  between operations  1.92 us (1%)
    pallas_call x1, Pallas kernels, shards(): pl.pallas_call(functools.partial(closing, rows, skip), out_shape=(jax.Sha...  55.9 us
    pallas_call x1, Pallas kernels, shards(): pl.pallas_call(functools.partial(opening, rows), out_shape=halo_shapes(he...  25 us
    dot_general x1, matrix products, shards(): dhidden = jnp.dot(g_out, w_out.T, preferred_element_type=jnp.float32)  6.65 us
    convert_element_type x1, other arithmetic, shards(): grad_image = (dblock + back).astype(b16)  6.56 us
    reduce_sum x1, other arithmetic, shards(): centre = conv - jnp.mean(conv, axis=-1, keepdims=True)  6.04 us
    dot_general x1, matrix products, shards(): pre = jnp.dot(normed, w_in, preferred_element_type=jnp.float32)  6.03 us
    reduce_sum x3, other arithmetic, shards(): jnp.sum(xpad[a:a + height, b:b + breadth] * dconv, axis=(0, 1))  5 us
    dot_general x1, matrix products, shards(): jnp.dot(hidden, w_out, preferred_element_type=jnp.float32)  4.23 us

profile of v2, /device:TPU:0, one launch (start us, length us, event | category | flops | bytes accessed | tf_op | source)
XLA Modules:
  0.0 142.5 jit_solution(9522434860848676325)
XLA Ops:
  0.6 0.8 eq.36
  1.4 1.5 %fusion.67 = (bf16[64,128]{1,0:T(8,128)(2,1)}, bf16[128]{0:T(256)(128)(2,1)S(1)}) fusion(s32[128]{0:T(128)} %param.14, s32[64]{0:T(128)S(1)} %eq.36), kind=kOutput, calls=%fused_computation.250 | convolution fusion | flops 2137984 | bytes 17408 | tf_op jit(solution)/shard_map/dot_general | solution.py:343
  2.9 0.7 reshape.109
  3.6 1.0 copy-done
  4.6 25.0 %opening.1 = (bf16[3,64,768]{2,1,0:T(8,128)(2,1)S(1)}, bf16[3,64,768]{2,1,0:T(8,128)(2,1)S(1)}, bf16[10,16,768]{2,1,0:T(8,128)(2,1)S(1)}, bf16[16,2,16,256]{3,2,1,0:T(8,128)(2,1)S(1)}) custom-call(bf16[4,64,768]{2,1,0:T(8,128)(2,1)S(1)} %copy-done, bf16[16,256]{1,0:T(8,128)(2,1)S(1)} %reshape.110.msg), custom_call_target="tpu_custom_call" | custom-call | tf_op jit(solution)/shard_map/opening/pallas_call | solution.py:349
  29.6 0.1 slice_select_fusion.3
  29.7 1.3 maximum_convert_fusion
  31.0 0.2 slice_reduce_fusion.47
  31.2 0.2 slice_reduce_fusion.48
  31.3 0.1 slice_reduce_fusion.46
  31.5 6.0 %fusion.66 = (f32[4,64]{1,0:T(4,128)S(1)}, f32[4,64,768]{2,1,0:T(8,128)S(1)}) fusion(f32[768]{0:T(1024)S(1)} %get-tuple-element.77, f32[10,70,768]{2,1,0:T(8,128)S(1)} %maximum_convert_fusion, f32[768]{0:T(1024)S(1)} %get-tuple-element.78, f32[768]{0:T(1024)S(1)} %get-tuple-element.79, f32[768]{0:T(1024)S(1)} %get-tuple-element.80, ...), kind=kLoop, calls=%fused_computation.249 | loop fusion | flops 19267328 | bytes 39473152 | tf_op jit(solution)/shard_map/reduce_sum | solution.py:374
  37.7 0.2 multiply_reduce_fusion.50
  37.9 0.1 fusion.55
  38.1 6.0 %multiply_convert_fusion = (bf16[256,3072]{1,0:T(8,128)(2,1)}, f32[256,3072]{1,0:T(8,128)}) fusion(bf16[256,768]{1,0:T(8,128)(2,1)S(1)} %bitcast.40, bf16[768,3072]{1,0:T(8,128)(2,1)} %param.10), kind=kOutput, calls=%fused_computation.9 | convolution fusion | flops 1211891712 | bytes 9830400 | tf_op jit(solution)/shard_map/dot_general | solution.py:378
  44.2 0.1 copy.13
  44.3 0.1 mul.1032
  44.4 0.1 div.49
  44.5 0.1 copy.14
  44.7 0.1 convert_element_type.82
  44.9 0.2 fusion.69
  45.2 6.7 %fusion = bf16[256,3072]{1,0:T(8,128)(2,1)S(1)} fusion(bf16[3072,768]{1,0:T(8,128)(2,1)} %param.11, f32[256,3072]{1,0:T(8,128)} %get-tuple-element.137, f32[256,768]{1,0:T(8,128)S(1)} %fusion.69, f32[768]{0:T(1024)S(1)} %copy-done.42), kind=kOutput, calls=%fused_computation.3 | convolution fusion | flops 1216217088 | bytes 10226688 | tf_op jit(solution)/shard_map/dot_general | solution.py:391
  52.0 2.3 %fusion.68 = (f32[256]{0:T(256)S(1)}, f32[256,768]{1,0:T(8,128)}) fusion(bf16[256,3072]{1,0:T(8,128)(2,1)S(1)} %fusion, bf16[768,3072]{1,0:T(8,128)(2,1)S(1)} %bitcast.52), kind=kOutput, calls=%fused_computation.251 | convolution fusion | flops 1208155904 | bytes 7078912 | tf_op jit(solution)/shard_map/dot_general | solution.py:396
  54.3 1.4 multiply_reduce_fusion.49
  55.7 0.1 div.59
  55.8 2.1 %fusion.65 = (bf16[4,64,768]{2,1,0:T(8,128)(2,1)}, f32[4,64,768]{2,1,0:T(8,128)S(1)}) fusion(f32[4,64]{1,0:T(4,128)S(1)} %broadcast_multiply_fusion, f32[4,64,768]{2,1,0:T(8,128)S(1)} %copy-done.3, f32[4,64]{1,0:T(4,128)S(1)} %broadcast_multiply_fusion.1, f32[4,64]{1,0:T(4,128)S(1)} %div.59, f32[256,768]{1,0:T(8,128)} %get-tuple-element.139, ...), kind=kLoop, calls=%fused_computation.248 | loop fusion | flops 1376256 | bytes 2756608 | tf_op jit(solution)/shard_map/convert_element_type | solution.py:426
  57.9 1.9 %multiply_reduce_fusion = (bf16[768]{0:T(1024)(128)(2,1)S(1)}, bf16[768]{0:T(1024)(128)(2,1)S(1)}, bf16[768]{0:T(1024)(128)(2,1)S(1)}, bf16[768]{0:T(1024)(128)(...) fusion(f32[4,64,768]{2,1,0:T(8,128)S(1)} %get-tuple-element.126, ...), kind=kLoop, calls=%fused_computation.113 | loop fusion | flops 7064064 | bytes 14969856 | tf_op jit(solution)/shard_map/reduce_sum | solution.py:407
  60.0 2.0 %multiply_reduce_fusion.18 = (bf16[768]{0:T(1024)(128)(2,1)S(1)}, bf16[768]{0:T(1024)(128)(2,1)S(1)}, bf16[768]{0:T(1024)(128)(2,1)S(1)}, bf16[768]{0:T(1024)(12...) fusion(f32[4,64,768]{2,1,0:T(8,128)S(1)} %get-tuple-element.126, ...), kind=kLoop, calls=%fused_computation.131 | loop fusion | flops 7064064 | bytes 14969856 | tf_op jit(solution)/shard_map/reduce_sum | solution.py:407
  62.2 1.1 multiply_reduce_fusion.36
  63.6 0.4 stack.249
  64.0 4.2 %fusion.70 = f32[256,768]{1,0:T(8,128)S(1)} fusion(bf16[256,3072]{1,0:T(8,128)(2,1)} %get-tuple-element.136, bf16[3072,768]{1,0:T(8,128)(2,1)} %param.11), kind=kOutput, calls=%fused_computation.253 | convolution fusion | flops 1207959552 | bytes 7077888 | tf_op jit(solution)/shard_map/dot_general | solution.py:381
  68.3 0.1 add_convert_fusion
  68.4 0.2 convolution_convert_fusion.2
  68.6 0.1 concatenate.27
  68.7 0.1 pad.18.clone
  68.8 0.9 maximum_maximum_fusion.ex
  69.7 3.6 %convolution_convert_fusion = bf16[3072,768]{1,0:T(8,128)(2,1)} fusion(bf16[256,3072]{1,0:T(8,128)(2,1)S(1)} %copy-done.6, bf16[256,768]{1,0:T(8,128)(2,1)S(1)} %bitcast.41), kind=kOutput, calls=%fused_computation | convolution fusion | flops 1210318848 | bytes 6684672 | tf_op jit(solution)/shard_map/dot_general | solution.py:394
  73.3 1.5 %convolution_convert_fusion.1 = bf16[3072,128]{1,0:T(8,128)(2,1)} fusion(bf16[256,3072]{1,0:T(8,128)(2,1)S(1)} %copy-done.11, bf16[256,128]{1,0:T(8,128)(2,1)S(1)} %bitcast.47), kind=kOutput, calls=%fused_computation.4 | convolution fusion | flops 201719808 | bytes 2424832 | tf_op jit(solution)/shard_map/dot_general | solution.py:395
  74.8 55.9 %closing.1 = (f32[96,768]{1,0:T(8,128)}, f32[96,128]{1,0:T(8,128)}, f32[16,384]{1,0:T(8,128)}, f32[16,2,8,384]{3,2,1,0:T(8,128)}, bf16[3,64,768]{2,1,0:T(8,128)(...) custom-call(bf16[16,2,96,768]{3,2,1,0:T(8,128)(2,1)} %bitcast.34, bf16[16,2,96,128]{3,2,1,0:T(8,128)(2,1)} %bitcast.35, ...), custom_call_target="tpu_custom_call" | custom-call | tf_op jit(solution)/shard_map/closing/pallas_call | solution.py:437
  130.8 0.1 reshape.122
  131.0 2.1 %fusion.57 = f32[96,768]{1,0:T(8,128)} fusion(f32[96,128]{1,0:T(8,128)} %get-tuple-element.25, f32[768]{0:T(1024)S(1)} %copy-done.43, f32[128,768]{1,0:T(8,128)S(1)} %reshape.122, f32[128]{0:T(128)S(1)} %copy-done.47), kind=kOutput, calls=%fused_computation.175 | convolution fusion | flops 113737728 | bytes 740864 | tf_op jit(solution)/shard_map/dot_general | solution.py:461
  133.1 0.1 slice_select_fusion.1
  133.2 0.3 maximum_convert_fusion.1
  133.6 6.6 %fusion.8 = bf16[4,64,768]{2,1,0:T(8,128)(2,1)} fusion(f32[4,64,768]{2,1,0:T(8,128)S(1)} %bitcast.36, f32[10,70,768]{2,1,0:T(8,128)S(1)} %maximum_convert_fusion.1, f32[768]{0:T(1024)S(1)} %get-tuple-element.77, f32[768]{0:T(1024)S(1)} %get-tuple-element.78, f32[768]{0:T(1024)S(1)} %get-tuple-element.79, f32[768]{0:T(1024)S(1)} %get-tuple-element.80, ...), kind=kLoop, calls=%fused_computation.18 | loop fusion | flops 19464192 | bytes 39865344 | tf_op jit(solution)/shard_map/convert_element_type | solution.py:465
  140.2 0.1 reshape.121
  140.3 0.7 slice.871
  141.0 0.1 dynamic-slice_multiply_fusion
  141.1 0.7 broadcast_divide_fusion
  141.8 0.7 copy.16
  (167 shorter events, 0.9 us)
Async XLA Ops:
  3.6 1.0 copy-start
  4.6 26.4 %copy-start.15 = (f32[49,768]{1,0:T(8,128)S(1)}, f32[49,768]{1,0:T(8,128)}, u32[]{:S(2)}) copy-start(f32[49,768]{1,0:T(8,128)} %param.9) | copy-start | bytes 451588
  31.4 6.2 %copy-start.18 = (f32[768]{0:T(1024)}, f32[768]{0:T(1024)S(1)}, u32[]{:S(2)}) copy-start(f32[768]{0:T(1024)S(1)} %get-tuple-element.115) | copy-start | bytes 9220
  31.5 6.1 %copy-start.20 = (f32[768]{0:T(1024)}, f32[768]{0:T(1024)S(1)}, u32[]{:S(2)}) copy-start(f32[768]{0:T(1024)S(1)} %get-tuple-element.116) | copy-start | bytes 9220
  31.5 6.1 %copy-start.22 = (f32[768]{0:T(1024)}, f32[768]{0:T(1024)S(1)}, u32[]{:S(2)}) copy-start(f32[768]{0:T(1024)S(1)} %get-tuple-element.117) | copy-start | bytes 9220
  31.5 6.1 %copy-start.24 = (f32[768]{0:T(1024)}, f32[768]{0:T(1024)S(1)}, u32[]{:S(2)}) copy-start(f32[768]{0:T(1024)S(1)} %get-tuple-element.118) | copy-start | bytes 9220
  31.5 6.1 %copy-start.26 = (f32[768]{0:T(1024)}, f32[768]{0:T(1024)S(1)}, u32[]{:S(2)}) copy-start(f32[768]{0:T(1024)S(1)} %get-tuple-element.119) | copy-start | bytes 9220
  31.5 6.1 %copy-start.28 = (f32[768]{0:T(1024)}, f32[768]{0:T(1024)S(1)}, u32[]{:S(2)}) copy-start(f32[768]{0:T(1024)S(1)} %get-tuple-element.120) | copy-start | bytes 9220
  31.5 6.1 %copy-start.30 = (f32[768]{0:T(1024)}, f32[768]{0:T(1024)S(1)}, u32[]{:S(2)}) copy-start(f32[768]{0:T(1024)S(1)} %get-tuple-element.121) | copy-start | bytes 9220
  31.5 6.1 %copy-start.32 = (f32[768]{0:T(1024)}, f32[768]{0:T(1024)S(1)}, u32[]{:S(2)}) copy-start(f32[768]{0:T(1024)S(1)} %get-tuple-element.122) | copy-start | bytes 9220
  31.5 6.1 %copy-start.34 = (f32[768]{0:T(1024)}, f32[768]{0:T(1024)S(1)}, u32[]{:S(2)}) copy-start(f32[768]{0:T(1024)S(1)} %get-tuple-element.123) | copy-start | bytes 9220
  31.5 6.1 %copy-start.36 = (f32[768]{0:T(1024)}, f32[768]{0:T(1024)S(1)}, u32[]{:S(2)}) copy-start(f32[768]{0:T(1024)S(1)} %get-tuple-element.124) | copy-start | bytes 9220
  37.7 6.5 %copy-start.2 = (f32[4,64,768]{2,1,0:T(8,128)}, f32[4,64,768]{2,1,0:T(8,128)S(1)}, u32[]{:S(2)}) copy-start(f32[4,64,768]{2,1,0:T(8,128)S(1)} %get-tuple-element.128) | copy-start | bytes 2359300
  37.9 6.2 %copy-start.38 = (f32[4,64]{1,0:T(4,128)}, f32[4,64]{1,0:T(4,128)S(1)}, u32[]{:S(2)}) copy-start(f32[4,64]{1,0:T(4,128)S(1)} %add_rsqrt_fusion) | copy-start | bytes 3076
  38.1 6.0 %copy-start.9 = (bf16[4,64,768]{2,1,0:T(8,128)(2,1)}, bf16[4,64,768]{2,1,0:T(8,128)(2,1)S(1)}, u32[]{:S(2)}) copy-start(bf16[4,64,768]{2,1,0:T(8,128)(2,1)S(1)} %fusion.55) | copy-start | bytes 1179652
  44.2 0.7 copy-start.40
  44.2 1.0 copy-start.42
  44.9 7.0 %slice-start = ((s8[4718592]{0:T(1024)(128)(4,1)}), s8[4194304]{0:T(1024)(128)(4,1)S(1)}, s32[]{:S(2)}) async-start(s8[4718592]{0:T(1024)(128)(4,1)} %bitcast.51), calls=%async_computation | async-start | bytes 8388608
  45.2 6.7 %copy-start.7 = (f32[256,768]{1,0:T(8,128)}, f32[256,768]{1,0:T(8,128)S(1)}, u32[]{:S(2)}) copy-start(f32[256,768]{1,0:T(8,128)S(1)} %fusion.69) | copy-start | bytes 2359300
  45.2 6.7 %slice-start.1 = ((s8[4718592]{0:T(1024)(128)(4,1)}), s8[524288]{0:T(1024)(128)(4,1)S(1)}, s32[]{:S(2)}) async-start(s8[4718592]{0:T(1024)(128)(4,1)} %bitcast.51), calls=%async_computation.1 | async-start | bytes 1048576
  51.9 2.3 %copy-start.5 = (bf16[256,3072]{1,0:T(8,128)(2,1)}, bf16[256,3072]{1,0:T(8,128)(2,1)S(1)}, u32[]{:S(2)}) copy-start(bf16[256,3072]{1,0:T(8,128)(2,1)S(1)} %fusion) | copy-start | bytes 4718596
  51.9 2.3 %copy-start.3 = (f32[4,64,768]{2,1,0:T(8,128)S(1)}, f32[4,64,768]{2,1,0:T(8,128)}, u32[]{:S(2)}) copy-start(f32[4,64,768]{2,1,0:T(8,128)} %copy-done.2) | copy-start | bytes 2359300
  51.9 2.3 %copy-start.39 = (f32[4,64]{1,0:T(4,128)S(1)}, f32[4,64]{1,0:T(4,128)}, u32[]{:S(2)}) copy-start(f32[4,64]{1,0:T(4,128)} %copy-done.38) | copy-start | bytes 3076
  64.0 4.3 %copy-start.1 = (bf16[4,64,768]{2,1,0:T(8,128)(2,1)S(1)}, bf16[4,64,768]{2,1,0:T(8,128)(2,1)}, u32[]{:S(2)}) copy-start(bf16[4,64,768]{2,1,0:T(8,128)(2,1)} %src.1) | copy-start | bytes 1179652
  64.0 4.3 %copy-start.43 = (f32[768]{0:T(1024)S(1)}, f32[768]{0:T(1024)}, u32[]{:S(2)}) copy-start(f32[768]{0:T(1024)} %param.12) | copy-start | bytes 9220
  68.3 1.4 copy-start.6
  68.3 1.5 %copy-start.10 = (bf16[4,64,768]{2,1,0:T(8,128)(2,1)S(1)}, bf16[4,64,768]{2,1,0:T(8,128)(2,1)}, u32[]{:S(2)}) copy-start(bf16[4,64,768]{2,1,0:T(8,128)(2,1)} %copy-done.9) | copy-start | bytes 1179652
  69.7 3.6 %copy-start.11 = (bf16[256,3072]{1,0:T(8,128)(2,1)S(1)}, bf16[256,3072]{1,0:T(8,128)(2,1)}, u32[]{:S(2)}) copy-start(bf16[256,3072]{1,0:T(8,128)(2,1)} %get-tuple-element.136) | copy-start | bytes 4718596
  74.8 56.1 %copy-start.47 = (f32[128]{0:T(128)S(1)}, f32[128]{0:T(128)}, u32[]{:S(2)}) copy-start(f32[128]{0:T(128)} %copy-done.46) | copy-start | bytes 1540
  130.7 2.4 %copy-start.17 = (bf16[10,16,768]{2,1,0:T(8,128)(2,1)S(1)}, bf16[10,16,768]{2,1,0:T(8,128)(2,1)}, u32[]{:S(2)}) copy-start(bf16[10,16,768]{2,1,0:T(8,128)(2,1)} %get-tuple-element.21) | copy-start | bytes 737284
  130.7 2.5 %copy-start.4 = (bf16[4,64,768]{2,1,0:T(8,128)(2,1)S(1)}, bf16[4,64,768]{2,1,0:T(8,128)(2,1)}, u32[]{:S(2)}) copy-start(bf16[4,64,768]{2,1,0:T(8,128)(2,1)} %get-tuple-element.125.src) | copy-start | bytes 1179652
  130.7 2.5 %copy-start.12 = (bf16[3,64,768]{2,1,0:T(8,128)(2,1)S(1)}, bf16[3,64,768]{2,1,0:T(8,128)(2,1)}, u32[]{:S(2)}) copy-start(bf16[3,64,768]{2,1,0:T(8,128)(2,1)} %get-tuple-element.22) | copy-start | bytes 884740
  130.7 2.5 %copy-start.13 = (bf16[3,64,768]{2,1,0:T(8,128)(2,1)S(1)}, bf16[3,64,768]{2,1,0:T(8,128)(2,1)}, u32[]{:S(2)}) copy-start(bf16[3,64,768]{2,1,0:T(8,128)(2,1)} %get-tuple-element.23) | copy-start | bytes 884740
  130.9 2.6 %copy-start.8 = (f32[256,768]{1,0:T(8,128)S(1)}, f32[256,768]{1,0:T(8,128)}, u32[]{:S(2)}) copy-start(f32[256,768]{1,0:T(8,128)} %copy-done.7) | copy-start | bytes 2359300
  130.9 2.6 %copy-start.19 = (f32[768]{0:T(1024)S(1)}, f32[768]{0:T(1024)}, u32[]{:S(2)}) copy-start(f32[768]{0:T(1024)} %copy-done.18) | copy-start | bytes 9220
  130.9 2.6 %copy-start.21 = (f32[768]{0:T(1024)S(1)}, f32[768]{0:T(1024)}, u32[]{:S(2)}) copy-start(f32[768]{0:T(1024)} %copy-done.20) | copy-start | bytes 9220
  130.9 2.6 %copy-start.23 = (f32[768]{0:T(1024)S(1)}, f32[768]{0:T(1024)}, u32[]{:S(2)}) copy-start(f32[768]{0:T(1024)} %copy-done.22) | copy-start | bytes 9220
  130.9 2.6 %copy-start.25 = (f32[768]{0:T(1024)S(1)}, f32[768]{0:T(1024)}, u32[]{:S(2)}) copy-start(f32[768]{0:T(1024)} %copy-done.24) | copy-start | bytes 9220
  131.0 2.6 %copy-start.27 = (f32[768]{0:T(1024)S(1)}, f32[768]{0:T(1024)}, u32[]{:S(2)}) copy-start(f32[768]{0:T(1024)} %copy-done.26) | copy-start | bytes 9220
  131.0 2.6 %copy-start.29 = (f32[768]{0:T(1024)S(1)}, f32[768]{0:T(1024)}, u32[]{:S(2)}) copy-start(f32[768]{0:T(1024)} %copy-done.28) | copy-start | bytes 9220
  131.0 2.6 %copy-start.31 = (f32[768]{0:T(1024)S(1)}, f32[768]{0:T(1024)}, u32[]{:S(2)}) copy-start(f32[768]{0:T(1024)} %copy-done.30) | copy-start | bytes 9220
  131.0 2.6 %copy-start.33 = (f32[768]{0:T(1024)S(1)}, f32[768]{0:T(1024)}, u32[]{:S(2)}) copy-start(f32[768]{0:T(1024)} %copy-done.32) | copy-start | bytes 9220
  131.0 2.6 %copy-start.35 = (f32[768]{0:T(1024)S(1)}, f32[768]{0:T(1024)}, u32[]{:S(2)}) copy-start(f32[768]{0:T(1024)} %copy-done.34) | copy-start | bytes 9220
  131.0 2.6 %copy-start.37 = (f32[768]{0:T(1024)S(1)}, f32[768]{0:T(1024)}, u32[]{:S(2)}) copy-start(f32[768]{0:T(1024)} %copy-done.36) | copy-start | bytes 9220
  133.6 6.6 %copy-start.16 = (f32[16,2,8,384]{3,2,1,0:T(8,128)S(1)}, f32[16,2,8,384]{3,2,1,0:T(8,128)}, u32[]{:S(2)}) copy-start(f32[16,2,8,384]{3,2,1,0:T(8,128)} %get-tuple-element.26) | copy-start | bytes 1179652
  133.6 7.4 %copy-start.41 = (f32[16,384]{1,0:T(8,128)S(1)}, f32[16,384]{1,0:T(8,128)}, u32[]{:S(2)}) copy-start(f32[16,384]{1,0:T(8,128)} %get-tuple-element.20) | copy-start | bytes 73732
  133.6 7.4 %copy-start.45 = (f32[128]{0:T(128)S(1)}, f32[128]{0:T(128)}, u32[]{:S(2)}) copy-start(f32[128]{0:T(128)} %copy-done.44) | copy-start | bytes 1540
  133.6 8.2 %copy-start.14 = (f32[96,768]{1,0:T(8,128)S(1)}, f32[96,768]{1,0:T(8,128)}, u32[]{:S(2)}) copy-start(f32[96,768]{1,0:T(8,128)} %get-tuple-element.24) | copy-start | bytes 884740
  (2 other events, 1.2 us)

commit v3 on v2

--- a/solution.py
+++ b/solution.py
@@ -37,13 +37,11 @@
             )
 
         self.up, self.down, self.side = up, down, side
-        self.to_down = [
-            copy(0, src.at[last], up, below, col),
-            copy(1, src.at[last, cols], side.at[pl.ds(0, 3)], below, 1 - col),
-        ]
-        self.to_up = [
-            copy(2, src.at[first], down, above, col),
-            copy(3, src.at[first, cols], side.at[pl.ds(h + 3, 3)], above, 1 - col),
+        self.to_down = [copy(0, src.at[last], up, below, col)]
+        self.to_up = [copy(2, src.at[first], down, above, col)]
+        self.corners = [
+            copy(1, up.at[:, cols], side.at[pl.ds(0, 3)], row, 1 - col),
+            copy(3, down.at[:, cols], side.at[pl.ds(h + 3, 3)], row, 1 - col),
         ]
         self.across = copy(4, src.at[:, cols], side.at[pl.ds(3, h)], row, 1 - col)
         self.h = h
@@ -81,30 +79,39 @@
         @pl.when(jnp.logical_not(self.has_up))
         def _():
             self.up[...] = jnp.zeros_like(self.up)
-            self.side[0:3] = jnp.zeros((3,) + self.side.shape[1:], self.side.dtype)
 
         @pl.when(jnp.logical_not(self.has_down))
         def _():
             self.down[...] = jnp.zeros_like(self.down)
-            self.side[self.h + 3 : self.h + 6] = jnp.zeros((3,) + self.side.shape[1:], self.side.dtype)
+
+    def relay(self):
+        @pl.when(self.has_down)
+        def _():
+            for c in self.to_up:
+                c.wait_recv()
+
+        @pl.when(self.has_up)
+        def _():
+            for c in self.to_down:
+                c.wait_recv()
+
+        for c in self.corners:
+            c.start()
 
     def finish(self):
-        self.across.wait_send()
-        self.across.wait_recv()
-
         @pl.when(self.has_down)
         def _():
             for c in self.to_down:
                 c.wait_send()
-            for c in self.to_up:
-                c.wait_recv()
 
         @pl.when(self.has_up)
         def _():
             for c in self.to_up:
                 c.wait_send()
-            for c in self.to_down:
-                c.wait_recv()
+
+        for c in [self.across] + self.corners:
+            c.wait_send()
+            c.wait_recv()
 
 
 def hop(src, dst, send, recv, row, col):
@@ -153,6 +160,7 @@
         copy.wait_recv()
     last = share(every, row, col, gs, gr)
     last.start()
+    halo.relay()
     halo.finish()
     last.wait_recv()
     for copy in copies + [last]:
@@ -276,6 +284,7 @@
             for copy in copies:
                 copy.wait_recv()
             last.start()
+            halo.relay()
     halo.finish()
     last.wait_recv()
     for copy in copies + tosses + [last, extra]:

time: 143 us -> 140 us (0.979)
  Pallas kernels: 80.9 us -> 77.6 us
    pallas_call x1, Pallas kernels: 55.9 us -> 54.1 us  [shards(): pl.pallas_call(functools.partial(closing, rows, skip), out_shape=(jax.Sha...]
    pallas_call x1, Pallas kernels: 25 us -> 23.5 us  [shards(): pl.pallas_call(functools.partial(opening, rows), out_shape=halo_shapes(he...]
where the time goes in v3:
time: 140 us; the launch traced here: 139 us
  Pallas kernels  77.6 us (55%)
  matrix products  28.3 us (20%)
  other arithmetic  25.1 us (18%)
  local copies, waits for them, and re-layouts  6.35 us (5%)
  between operations  1.92 us (1%)
    pallas_call x1, Pallas kernels, shards(): pl.pallas_call(functools.partial(closing, rows, skip), out_shape=(jax.Sha...  54.1 us
    pallas_call x1, Pallas kernels, shards(): pl.pallas_call(functools.partial(opening, rows), out_shape=halo_shapes(he...  23.5 us
    dot_general x1, matrix products, shards(): dhidden = jnp.dot(g_out, w_out.T, preferred_element_type=jnp.float32)  6.65 us
    convert_element_type x1, other arithmetic, shards(): grad_image = (dblock + back).astype(b16)  6.56 us
    reduce_sum x1, other arithmetic, shards(): centre = conv - jnp.mean(conv, axis=-1, keepdims=True)  6.04 us
    dot_general x1, matrix products, shards(): pre = jnp.dot(normed, w_in, preferred_element_type=jnp.float32)  6.03 us
    reduce_sum x3, other arithmetic, shards(): jnp.sum(xpad[a:a + height, b:b + breadth] * dconv, axis=(0, 1))  5 us
    dot_general x1, matrix products, shards(): jnp.dot(hidden, w_out, preferred_element_type=jnp.float32)  4.23 us

profile of v3, /device:TPU:0, one launch (start us, length us, event | category | flops | bytes accessed | tf_op | source)
XLA Modules:
  0.0 139.2 jit_solution(8679629226350708583)
XLA Ops:
  0.6 0.8 eq.36
  1.4 1.5 %fusion.67 = (bf16[64,128]{1,0:T(8,128)(2,1)}, bf16[128]{0:T(256)(128)(2,1)S(1)}) fusion(s32[128]{0:T(128)} %param.14, s32[64]{0:T(128)S(1)} %eq.36), kind=kOutput, calls=%fused_computation.250 | convolution fusion | flops 2137984 | bytes 17408 | tf_op jit(solution)/shard_map/dot_general | solution.py:352
  2.9 0.7 reshape.109
  3.6 1.0 copy-done
  4.6 23.5 %opening.1 = (bf16[3,64,768]{2,1,0:T(8,128)(2,1)S(1)}, bf16[3,64,768]{2,1,0:T(8,128)(2,1)S(1)}, bf16[10,16,768]{2,1,0:T(8,128)(2,1)S(1)}, bf16[16,2,16,256]{3,2,1,0:T(8,128)(2,1)S(1)}) custom-call(bf16[4,64,768]{2,1,0:T(8,128)(2,1)S(1)} %copy-done, bf16[16,256]{1,0:T(8,128)(2,1)S(1)} %reshape.110.msg), custom_call_target="tpu_custom_call" | custom-call | tf_op jit(solution)/shard_map/opening/pallas_call | solution.py:358
  28.1 0.1 slice_select_fusion.3
  28.2 1.3 maximum_convert_fusion
  29.5 0.2 slice_reduce_fusion.47
  29.6 0.2 slice_reduce_fusion.48
  29.8 0.1 slice_reduce_fusion.46
  30.0 6.0 %fusion.66 = (f32[4,64]{1,0:T(4,128)S(1)}, f32[4,64,768]{2,1,0:T(8,128)S(1)}) fusion(f32[768]{0:T(1024)S(1)} %get-tuple-element.77, f32[10,70,768]{2,1,0:T(8,128)S(1)} %maximum_convert_fusion, f32[768]{0:T(1024)S(1)} %get-tuple-element.78, f32[768]{0:T(1024)S(1)} %get-tuple-element.79, f32[768]{0:T(1024)S(1)} %get-tuple-element.80, ...), kind=kLoop, calls=%fused_computation.249 | loop fusion | flops 19267328 | bytes 39473152 | tf_op jit(solution)/shard_map/reduce_sum | solution.py:383
  36.2 0.2 multiply_reduce_fusion.50
  36.4 0.1 fusion.55
  36.6 6.0 %multiply_convert_fusion = (bf16[256,3072]{1,0:T(8,128)(2,1)}, f32[256,3072]{1,0:T(8,128)}) fusion(bf16[256,768]{1,0:T(8,128)(2,1)S(1)} %bitcast.40, bf16[768,3072]{1,0:T(8,128)(2,1)} %param.10), kind=kOutput, calls=%fused_computation.9 | convolution fusion | flops 1211891712 | bytes 9830400 | tf_op jit(solution)/shard_map/dot_general | solution.py:387
  42.7 0.1 copy.13
  42.8 0.1 mul.1032
  42.9 0.1 div.49
  43.0 0.1 copy.14
  43.2 0.1 convert_element_type.82
  43.4 0.2 fusion.69
  43.7 6.7 %fusion = bf16[256,3072]{1,0:T(8,128)(2,1)S(1)} fusion(bf16[3072,768]{1,0:T(8,128)(2,1)} %param.11, f32[256,3072]{1,0:T(8,128)} %get-tuple-element.137, f32[256,768]{1,0:T(8,128)S(1)} %fusion.69, f32[768]{0:T(1024)S(1)} %copy-done.42), kind=kOutput, calls=%fused_computation.3 | convolution fusion | flops 1216217088 | bytes 10226688 | tf_op jit(solution)/shard_map/dot_general | solution.py:400
  50.4 2.3 %fusion.68 = (f32[256]{0:T(256)S(1)}, f32[256,768]{1,0:T(8,128)}) fusion(bf16[256,3072]{1,0:T(8,128)(2,1)S(1)} %fusion, bf16[768,3072]{1,0:T(8,128)(2,1)S(1)} %bitcast.52), kind=kOutput, calls=%fused_computation.251 | convolution fusion | flops 1208155904 | bytes 7078912 | tf_op jit(solution)/shard_map/dot_general | solution.py:405
  52.7 1.4 multiply_reduce_fusion.49
  54.2 0.1 div.59
  54.2 2.1 %fusion.65 = (bf16[4,64,768]{2,1,0:T(8,128)(2,1)}, f32[4,64,768]{2,1,0:T(8,128)S(1)}) fusion(f32[4,64]{1,0:T(4,128)S(1)} %broadcast_multiply_fusion, f32[4,64,768]{2,1,0:T(8,128)S(1)} %copy-done.3, f32[4,64]{1,0:T(4,128)S(1)} %broadcast_multiply_fusion.1, f32[4,64]{1,0:T(4,128)S(1)} %div.59, f32[256,768]{1,0:T(8,128)} %get-tuple-element.139, ...), kind=kLoop, calls=%fused_computation.248 | loop fusion | flops 1376256 | bytes 2756608 | tf_op jit(solution)/shard_map/convert_element_type | solution.py:435
  56.4 1.9 %multiply_reduce_fusion = (bf16[768]{0:T(1024)(128)(2,1)S(1)}, bf16[768]{0:T(1024)(128)(2,1)S(1)}, bf16[768]{0:T(1024)(128)(2,1)S(1)}, bf16[768]{0:T(1024)(128)(...) fusion(f32[4,64,768]{2,1,0:T(8,128)S(1)} %get-tuple-element.126, ...), kind=kLoop, calls=%fused_computation.113 | loop fusion | flops 7064064 | bytes 14969856 | tf_op jit(solution)/shard_map/reduce_sum | solution.py:416
  58.5 2.0 %multiply_reduce_fusion.18 = (bf16[768]{0:T(1024)(128)(2,1)S(1)}, bf16[768]{0:T(1024)(128)(2,1)S(1)}, bf16[768]{0:T(1024)(128)(2,1)S(1)}, bf16[768]{0:T(1024)(12...) fusion(f32[4,64,768]{2,1,0:T(8,128)S(1)} %get-tuple-element.126, ...), kind=kLoop, calls=%fused_computation.131 | loop fusion | flops 7064064 | bytes 14969856 | tf_op jit(solution)/shard_map/reduce_sum | solution.py:416
  60.7 1.1 multiply_reduce_fusion.36
  62.0 0.4 stack.249
  62.5 4.2 %fusion.70 = f32[256,768]{1,0:T(8,128)S(1)} fusion(bf16[256,3072]{1,0:T(8,128)(2,1)} %get-tuple-element.136, bf16[3072,768]{1,0:T(8,128)(2,1)} %param.11), kind=kOutput, calls=%fused_computation.253 | convolution fusion | flops 1207959552 | bytes 7077888 | tf_op jit(solution)/shard_map/dot_general | solution.py:390
  66.8 0.1 add_convert_fusion
  66.9 0.2 convolution_convert_fusion.2
  67.1 0.1 concatenate.27
  67.2 0.1 pad.18.clone
  67.3 0.9 maximum_maximum_fusion.ex
  68.2 3.6 %convolution_convert_fusion = bf16[3072,768]{1,0:T(8,128)(2,1)} fusion(bf16[256,3072]{1,0:T(8,128)(2,1)S(1)} %copy-done.6, bf16[256,768]{1,0:T(8,128)(2,1)S(1)} %bitcast.41), kind=kOutput, calls=%fused_computation | convolution fusion | flops 1210318848 | bytes 6684672 | tf_op jit(solution)/shard_map/dot_general | solution.py:403
  71.8 1.5 %convolution_convert_fusion.1 = bf16[3072,128]{1,0:T(8,128)(2,1)} fusion(bf16[256,3072]{1,0:T(8,128)(2,1)S(1)} %copy-done.11, bf16[256,128]{1,0:T(8,128)(2,1)S(1)} %bitcast.47), kind=kOutput, calls=%fused_computation.4 | convolution fusion | flops 201719808 | bytes 2424832 | tf_op jit(solution)/shard_map/dot_general | solution.py:404
  73.3 54.1 %closing.1 = (f32[96,768]{1,0:T(8,128)}, f32[96,128]{1,0:T(8,128)}, f32[16,384]{1,0:T(8,128)}, f32[16,2,8,384]{3,2,1,0:T(8,128)}, bf16[3,64,768]{2,1,0:T(8,128)(...) custom-call(bf16[16,2,96,768]{3,2,1,0:T(8,128)(2,1)} %bitcast.34, bf16[16,2,96,128]{3,2,1,0:T(8,128)(2,1)} %bitcast.35, ...), custom_call_target="tpu_custom_call" | custom-call | tf_op jit(solution)/shard_map/closing/pallas_call | solution.py:446
  127.5 0.1 reshape.122
  127.7 2.1 %fusion.57 = f32[96,768]{1,0:T(8,128)} fusion(f32[96,128]{1,0:T(8,128)} %get-tuple-element.25, f32[768]{0:T(1024)S(1)} %copy-done.43, f32[128,768]{1,0:T(8,128)S(1)} %reshape.122, f32[128]{0:T(128)S(1)} %copy-done.47), kind=kOutput, calls=%fused_computation.175 | convolution fusion | flops 113737728 | bytes 740864 | tf_op jit(solution)/shard_map/dot_general | solution.py:470
  129.8 0.1 slice_select_fusion.1
  129.9 0.3 maximum_convert_fusion.1
  130.4 6.6 %fusion.8 = bf16[4,64,768]{2,1,0:T(8,128)(2,1)} fusion(f32[4,64,768]{2,1,0:T(8,128)S(1)} %bitcast.36, f32[10,70,768]{2,1,0:T(8,128)S(1)} %maximum_convert_fusion.1, f32[768]{0:T(1024)S(1)} %get-tuple-element.77, f32[768]{0:T(1024)S(1)} %get-tuple-element.78, f32[768]{0:T(1024)S(1)} %get-tuple-element.79, f32[768]{0:T(1024)S(1)} %get-tuple-element.80, ...), kind=kLoop, calls=%fused_computation.18 | loop fusion | flops 19464192 | bytes 39865344 | tf_op jit(solution)/shard_map/convert_element_type | solution.py:474
  136.9 0.1 reshape.121
  137.1 0.7 slice.871
  137.8 0.1 dynamic-slice_multiply_fusion
  137.8 0.7 broadcast_divide_fusion
  138.5 0.7 copy.16
  (167 shorter events, 0.9 us)
Async XLA Ops:
  3.6 1.0 copy-start
  4.6 24.9 %copy-start.15 = (f32[49,768]{1,0:T(8,128)S(1)}, f32[49,768]{1,0:T(8,128)}, u32[]{:S(2)}) copy-start(f32[49,768]{1,0:T(8,128)} %param.9) | copy-start | bytes 451588
  29.9 6.2 %copy-start.18 = (f32[768]{0:T(1024)}, f32[768]{0:T(1024)S(1)}, u32[]{:S(2)}) copy-start(f32[768]{0:T(1024)S(1)} %get-tuple-element.115) | copy-start | bytes 9220
  29.9 6.1 %copy-start.20 = (f32[768]{0:T(1024)}, f32[768]{0:T(1024)S(1)}, u32[]{:S(2)}) copy-start(f32[768]{0:T(1024)S(1)} %get-tuple-element.116) | copy-start | bytes 9220
  29.9 6.1 %copy-start.22 = (f32[768]{0:T(1024)}, f32[768]{0:T(1024)S(1)}, u32[]{:S(2)}) copy-start(f32[768]{0:T(1024)S(1)} %get-tuple-element.117) | copy-start | bytes 9220
  30.0 6.1 %copy-start.24 = (f32[768]{0:T(1024)}, f32[768]{0:T(1024)S(1)}, u32[]{:S(2)}) copy-start(f32[768]{0:T(1024)S(1)} %get-tuple-element.118) | copy-start | bytes 9220
  30.0 6.1 %copy-start.26 = (f32[768]{0:T(1024)}, f32[768]{0:T(1024)S(1)}, u32[]{:S(2)}) copy-start(f32[768]{0:T(1024)S(1)} %get-tuple-element.119) | copy-start | bytes 9220
  30.0 6.1 %copy-start.28 = (f32[768]{0:T(1024)}, f32[768]{0:T(1024)S(1)}, u32[]{:S(2)}) copy-start(f32[768]{0:T(1024)S(1)} %get-tuple-element.120) | copy-start | bytes 9220
  30.0 6.1 %copy-start.30 = (f32[768]{0:T(1024)}, f32[768]{0:T(1024)S(1)}, u32[]{:S(2)}) copy-start(f32[768]{0:T(1024)S(1)} %get-tuple-element.121) | copy-start | bytes 9220
  30.0 6.1 %copy-start.32 = (f32[768]{0:T(1024)}, f32[768]{0:T(1024)S(1)}, u32[]{:S(2)}) copy-start(f32[768]{0:T(1024)S(1)} %get-tuple-element.122) | copy-start | bytes 9220
  30.0 6.1 %copy-start.34 = (f32[768]{0:T(1024)}, f32[768]{0:T(1024)S(1)}, u32[]{:S(2)}) copy-start(f32[768]{0:T(1024)S(1)} %get-tuple-element.123) | copy-start | bytes 9220
  30.0 6.1 %copy-start.36 = (f32[768]{0:T(1024)}, f32[768]{0:T(1024)S(1)}, u32[]{:S(2)}) copy-start(f32[768]{0:T(1024)S(1)} %get-tuple-element.124) | copy-start | bytes 9220
  36.2 6.5 %copy-start.2 = (f32[4,64,768]{2,1,0:T(8,128)}, f32[4,64,768]{2,1,0:T(8,128)S(1)}, u32[]{:S(2)}) copy-start(f32[4,64,768]{2,1,0:T(8,128)S(1)} %get-tuple-element.128) | copy-start | bytes 2359300
  36.4 6.2 %copy-start.38 = (f32[4,64]{1,0:T(4,128)}, f32[4,64]{1,0:T(4,128)S(1)}, u32[]{:S(2)}) copy-start(f32[4,64]{1,0:T(4,128)S(1)} %add_rsqrt_fusion) | copy-start | bytes 3076
  36.6 6.0 %copy-start.9 = (bf16[4,64,768]{2,1,0:T(8,128)(2,1)}, bf16[4,64,768]{2,1,0:T(8,128)(2,1)S(1)}, u32[]{:S(2)}) copy-start(bf16[4,64,768]{2,1,0:T(8,128)(2,1)S(1)} %fusion.55) | copy-start | bytes 1179652
  42.6 0.7 copy-start.40
  42.6 1.0 copy-start.42
  43.4 7.0 %slice-start = ((s8[4718592]{0:T(1024)(128)(4,1)}), s8[4194304]{0:T(1024)(128)(4,1)S(1)}, s32[]{:S(2)}) async-start(s8[4718592]{0:T(1024)(128)(4,1)} %bitcast.51), calls=%async_computation | async-start | bytes 8388608
  43.7 6.7 %copy-start.7 = (f32[256,768]{1,0:T(8,128)}, f32[256,768]{1,0:T(8,128)S(1)}, u32[]{:S(2)}) copy-start(f32[256,768]{1,0:T(8,128)S(1)} %fusion.69) | copy-start | bytes 2359300
  43.7 6.7 %slice-start.1 = ((s8[4718592]{0:T(1024)(128)(4,1)}), s8[524288]{0:T(1024)(128)(4,1)S(1)}, s32[]{:S(2)}) async-start(s8[4718592]{0:T(1024)(128)(4,1)} %bitcast.51), calls=%async_computation.1 | async-start | bytes 1048576
  50.4 2.3 %copy-start.5 = (bf16[256,3072]{1,0:T(8,128)(2,1)}, bf16[256,3072]{1,0:T(8,128)(2,1)S(1)}, u32[]{:S(2)}) copy-start(bf16[256,3072]{1,0:T(8,128)(2,1)S(1)} %fusion) | copy-start | bytes 4718596
  50.4 2.3 %copy-start.3 = (f32[4,64,768]{2,1,0:T(8,128)S(1)}, f32[4,64,768]{2,1,0:T(8,128)}, u32[]{:S(2)}) copy-start(f32[4,64,768]{2,1,0:T(8,128)} %copy-done.2) | copy-start | bytes 2359300
  50.4 2.3 %copy-start.39 = (f32[4,64]{1,0:T(4,128)S(1)}, f32[4,64]{1,0:T(4,128)}, u32[]{:S(2)}) copy-start(f32[4,64]{1,0:T(4,128)} %copy-done.38) | copy-start | bytes 3076
  62.5 4.3 %copy-start.1 = (bf16[4,64,768]{2,1,0:T(8,128)(2,1)S(1)}, bf16[4,64,768]{2,1,0:T(8,128)(2,1)}, u32[]{:S(2)}) copy-start(bf16[4,64,768]{2,1,0:T(8,128)(2,1)} %src.1) | copy-start | bytes 1179652
  62.5 4.3 %copy-start.43 = (f32[768]{0:T(1024)S(1)}, f32[768]{0:T(1024)}, u32[]{:S(2)}) copy-start(f32[768]{0:T(1024)} %param.12) | copy-start | bytes 9220
  66.7 1.4 %copy-start.6 = (bf16[256,3072]{1,0:T(8,128)(2,1)S(1)}, bf16[256,3072]{1,0:T(8,128)(2,1)}, u32[]{:S(2)}) copy-start(bf16[256,3072]{1,0:T(8,128)(2,1)} %copy-done.5) | copy-start | bytes 4718596
  66.7 1.5 %copy-start.10 = (bf16[4,64,768]{2,1,0:T(8,128)(2,1)S(1)}, bf16[4,64,768]{2,1,0:T(8,128)(2,1)}, u32[]{:S(2)}) copy-start(bf16[4,64,768]{2,1,0:T(8,128)(2,1)} %copy-done.9) | copy-start | bytes 1179652
  68.2 3.6 %copy-start.11 = (bf16[256,3072]{1,0:T(8,128)(2,1)S(1)}, bf16[256,3072]{1,0:T(8,128)(2,1)}, u32[]{:S(2)}) copy-start(bf16[256,3072]{1,0:T(8,128)(2,1)} %get-tuple-element.136) | copy-start | bytes 4718596
  73.3 54.3 %copy-start.47 = (f32[128]{0:T(128)S(1)}, f32[128]{0:T(128)}, u32[]{:S(2)}) copy-start(f32[128]{0:T(128)} %copy-done.46) | copy-start | bytes 1540
  127.4 2.4 %copy-start.17 = (bf16[10,16,768]{2,1,0:T(8,128)(2,1)S(1)}, bf16[10,16,768]{2,1,0:T(8,128)(2,1)}, u32[]{:S(2)}) copy-start(bf16[10,16,768]{2,1,0:T(8,128)(2,1)} %get-tuple-element.21) | copy-start | bytes 737284
  127.4 2.5 %copy-start.4 = (bf16[4,64,768]{2,1,0:T(8,128)(2,1)S(1)}, bf16[4,64,768]{2,1,0:T(8,128)(2,1)}, u32[]{:S(2)}) copy-start(bf16[4,64,768]{2,1,0:T(8,128)(2,1)} %get-tuple-element.125.src) | copy-start | bytes 1179652
  127.4 2.5 %copy-start.12 = (bf16[3,64,768]{2,1,0:T(8,128)(2,1)S(1)}, bf16[3,64,768]{2,1,0:T(8,128)(2,1)}, u32[]{:S(2)}) copy-start(bf16[3,64,768]{2,1,0:T(8,128)(2,1)} %get-tuple-element.22) | copy-start | bytes 884740
  127.5 2.5 %copy-start.13 = (bf16[3,64,768]{2,1,0:T(8,128)(2,1)S(1)}, bf16[3,64,768]{2,1,0:T(8,128)(2,1)}, u32[]{:S(2)}) copy-start(bf16[3,64,768]{2,1,0:T(8,128)(2,1)} %get-tuple-element.23) | copy-start | bytes 884740
  127.6 2.6 %copy-start.8 = (f32[256,768]{1,0:T(8,128)S(1)}, f32[256,768]{1,0:T(8,128)}, u32[]{:S(2)}) copy-start(f32[256,768]{1,0:T(8,128)} %copy-done.7) | copy-start | bytes 2359300
  127.6 2.6 %copy-start.19 = (f32[768]{0:T(1024)S(1)}, f32[768]{0:T(1024)}, u32[]{:S(2)}) copy-start(f32[768]{0:T(1024)} %copy-done.18) | copy-start | bytes 9220
  127.7 2.6 %copy-start.21 = (f32[768]{0:T(1024)S(1)}, f32[768]{0:T(1024)}, u32[]{:S(2)}) copy-start(f32[768]{0:T(1024)} %copy-done.20) | copy-start | bytes 9220
  127.7 2.6 %copy-start.23 = (f32[768]{0:T(1024)S(1)}, f32[768]{0:T(1024)}, u32[]{:S(2)}) copy-start(f32[768]{0:T(1024)} %copy-done.22) | copy-start | bytes 9220
  127.7 2.6 %copy-start.25 = (f32[768]{0:T(1024)S(1)}, f32[768]{0:T(1024)}, u32[]{:S(2)}) copy-start(f32[768]{0:T(1024)} %copy-done.24) | copy-start | bytes 9220
  127.7 2.6 %copy-start.27 = (f32[768]{0:T(1024)S(1)}, f32[768]{0:T(1024)}, u32[]{:S(2)}) copy-start(f32[768]{0:T(1024)} %copy-done.26) | copy-start | bytes 9220
  127.7 2.6 %copy-start.29 = (f32[768]{0:T(1024)S(1)}, f32[768]{0:T(1024)}, u32[]{:S(2)}) copy-start(f32[768]{0:T(1024)} %copy-done.28) | copy-start | bytes 9220
  127.7 2.6 %copy-start.31 = (f32[768]{0:T(1024)S(1)}, f32[768]{0:T(1024)}, u32[]{:S(2)}) copy-start(f32[768]{0:T(1024)} %copy-done.30) | copy-start | bytes 9220
  127.7 2.6 %copy-start.33 = (f32[768]{0:T(1024)S(1)}, f32[768]{0:T(1024)}, u32[]{:S(2)}) copy-start(f32[768]{0:T(1024)} %copy-done.32) | copy-start | bytes 9220
  127.7 2.6 %copy-start.35 = (f32[768]{0:T(1024)S(1)}, f32[768]{0:T(1024)}, u32[]{:S(2)}) copy-start(f32[768]{0:T(1024)} %copy-done.34) | copy-start | bytes 9220
  127.7 2.6 %copy-start.37 = (f32[768]{0:T(1024)S(1)}, f32[768]{0:T(1024)}, u32[]{:S(2)}) copy-start(f32[768]{0:T(1024)} %copy-done.36) | copy-start | bytes 9220
  130.3 6.6 %copy-start.16 = (f32[16,2,8,384]{3,2,1,0:T(8,128)S(1)}, f32[16,2,8,384]{3,2,1,0:T(8,128)}, u32[]{:S(2)}) copy-start(f32[16,2,8,384]{3,2,1,0:T(8,128)} %get-tuple-element.26) | copy-start | bytes 1179652
  130.3 7.4 %copy-start.41 = (f32[16,384]{1,0:T(8,128)S(1)}, f32[16,384]{1,0:T(8,128)}, u32[]{:S(2)}) copy-start(f32[16,384]{1,0:T(8,128)} %get-tuple-element.20) | copy-start | bytes 73732
  130.3 7.4 %copy-start.45 = (f32[128]{0:T(128)S(1)}, f32[128]{0:T(128)}, u32[]{:S(2)}) copy-start(f32[128]{0:T(128)} %copy-done.44) | copy-start | bytes 1540
  130.3 8.2 %copy-start.14 = (f32[96,768]{1,0:T(8,128)S(1)}, f32[96,768]{1,0:T(8,128)}, u32[]{:S(2)}) copy-start(f32[96,768]{1,0:T(8,128)} %get-tuple-element.24) | copy-start | bytes 884740
  (2 other events, 1.2 us)
